TPU v7x, 256 devices: a whole 4x4x8 slice. The times are simulated.
256 devices in a mesh: row: 32 (over y_hi, z, core), col: 8 (over y_lo, x).
Axes of the slice: x: 4, y: 4 (y_hi: 2, y_lo: 2; y = y_hi * 2 + y_lo), z: 8, core: 2. Of those that a mesh axis runs over, the one named last changes fastest.
Arguments:
- left_panel: float32 [8192, 512], P('row', 'col'), may hold values from -0.25 to 0.25
- accum: float32 [8192, 8192], P('row', 'col'), may hold values from -6 to 6
- col_scale: float32 [8192], P('col'), may hold values from 0.3 to 3
Outputs:
- scaled_square: float32 [8192, 8192], P('row', 'col')
All inputs are finite; a program needn't handle non-finite values.
Results may differ from a plain program's by a relative error of at most 0.00005.
Values sent between devices are 32-bit elements; how exact they have to be, the bound alone decides.
No kernel may reach another device: no remote copies, remote signals or barrier semaphores. Data moves between devices by JAX's collectives and lax.ppermute only.
A program may use at most 64 MiB of HBM per device.

v0:
```python
import jax
import jax.numpy as jnp
from jax import lax
from jax.sharding import PartitionSpec as P


def per_device(left_panel, accum, col_scale):
    cols_dev = accum.shape[1]
    full_rows = lax.all_gather(left_panel, "col", axis=1, tiled=True)
    everyone = lax.all_gather(full_rows, "row", axis=0, tiled=True)
    mirror = lax.dynamic_slice_in_dim(everyone, lax.axis_index("col") * cols_dev, cols_dev, 0)
    mixed = accum + lax.dot_general(
        full_rows,
        mirror,
        (((1,), (1,)), ((), ())),
        precision=lax.Precision.HIGHEST,
        preferred_element_type=jnp.float32,
    )
    scaled = mixed * col_scale[None, :]
    totals = lax.psum(jnp.sum(scaled * scaled, axis=1), "col")
    count = cols_dev * lax.axis_size("col")
    return scaled * lax.rsqrt(totals / count + 1e-06)[:, None]


def solution(mesh):
    placed = (P("row", "col"), P("row", "col"), P("col"))
    return jax.shard_map(
        per_device, mesh=mesh, in_specs=placed, out_specs=P("row", "col"), check_vma=False
    )
```

profile of v0, /device:TPU:1, one launch (start us, length us, event | category | flops | bytes accessed | tf_op | source)
XLA Modules:
  0.0 223.0 jit_solution(4452210736035881062)
XLA Ops:
  6.5 0.0 all-gather.2.cloned.1.call-start
  6.5 26.5 %all_gather.6 = f32[256,512]{0,1:T(8,128)} all-gather(f32[256,64]{0,1:T(8,128)} %param.3), channel_id=1, replica_groups=mesh['row'=32,'col'=8] {'col'}, dimensions={1}, use_global_device_ids=true | all-gather | bytes 589824 | tf_op jit(solution)/shard_map/all_gather | solution.py:9
  33.0 0.0 all-gather.2.cloned.1.call-update
  33.1 1.6 copy.4
  34.6 159.9 %all-gather.2.cloned.1.call-done = f32[8192,512]{0,1:T(8,128)} async-done(((f32[256,512]{0,1:T(8,128)}), f32[8192,512]{0,1:T(8,128)}) %all-gather.2.cloned.1.call-update) | async-done | bytes 16777232 | tf_op jit(solution)/shard_map/all_gather | solution.py:10
  194.5 5.3 %multiply_reduce_fusion = (f32[256]{0:T(256)S(1)}, f32[256,1024]{0,1:T(8,128)S(1)}) fusion(f32[1024]{0:T(1024)} %param.5, f32[256,1024]{0,1:T(8,128)S(1)} %copy.4, f32[256,512]{0,1:T(8,128)} %all_gather.6, f32[8192,512]{0,1:T(8,128)} %all-gather.2.cloned.1.call-done, s32[]{:T(128)S(6)} %select_n.3), kind=kOutput, calls=%fused_computation.5 | convolution fusion | flops 1611661056 | bytes 4723716 | tf_op jit(solution)/shard_map/dot_general | solution.py:12
  199.8 14.9 %psum.7 = f32[256]{0:T(256)S(1)} all-reduce(f32[256]{0:T(256)S(1)} %get-tuple-element.5), channel_id=1, replica_groups=mesh['row'=32,'col'=8] {'col'}, use_global_device_ids=true, to_apply=%region_1.0 | all-reduce | flops 256 | bytes 2048 | tf_op jit(solution)/shard_map/psum | solution.py:20
  214.8 0.1 broadcast_multiply_fusion
  214.8 1.3 copy.5
  (1 shorter events, 0.0 us)
Async XLA Ops:
  6.5 188.0 %all-gather.2.cloned.1.call-start = ((), (), s32[]{:S(2)}) async-start(), calls=%async_computation | async-start | bytes 17301504 | tf_op jit(solution)/shard_map/all_gather | solution.py:10
Sparse Core Ops, SparseCore 0:
  33.2 161.3 all-gather.1
where the time goes:
time: 226 us; the launch traced here: 223 us
  waiting for transfers between devices  160 us (71%)
  blocking collectives  41.4 us (18%)
  between operations  13.4 us (6%)
  matrix products  5.3 us (2%)
  local copies, waits for them, and re-layouts  2.86 us (1%)
    all_gather x1, waiting for transfers between devices, per_device(): everyone = lax.all_gather(full_rows, 'row', axis=0, tiled=True)  160 us
    all_gather x1, blocking collectives, per_device(): full_rows = lax.all_gather(left_panel, 'col', axis=1, tiled=True)  26.5 us
    psum x1, blocking collectives, per_device(): totals = lax.psum(jnp.sum(scaled * scaled, axis=1), 'col')  14.9 us
    dot_general x1, matrix products, per_device(): lax.dot_general(full_rows, mirror, (((1,), (1,)), ((), ())), precision=la...  5.3 us
  transfers between devices with their start and end apart: 1, of which 1 were waited for; matrix products, arithmetic and copies ran while one was open for 1% of the time, Pallas kernels for 0%

commit v1 on v0

v1 whole, which is shorter than its diff:
```python
import jax
import jax.numpy as jnp
from jax import lax
from jax.experimental import pallas as pl
from jax.experimental.pallas import tpu as pltpu
from jax.sharding import Mesh, PartitionSpec as P

YH, Z, CORE, YL, X = 2, 8, 2, 2, 4
ROW = ("yh", "z", "core")
COL = ("yl", "x")
VMEM = pl.BlockSpec(memory_space=pltpu.VMEM)
SMEM = pl.BlockSpec(memory_space=pltpu.SMEM)


def along_z(shift):
    pairs = []
    for yh in range(YH):
        for z in range(Z):
            for yl in range(YL):
                source = (yh * Z + z) * YL + yl
                target = (yl * Z + (z + shift) % Z) * YL + yh
                pairs.append((source, target))
    return pairs


def sort_planes(z_ref, *refs):
    pieces, out_ref = refs[:-1], refs[-1]
    for shift, piece in enumerate(pieces):
        plane = lax.rem(z_ref[0] + Z - shift, Z)
        value = piece[...]
        for copy in range(YH):
            out_ref[copy, plane] = value


def split(value):
    high = value.astype(jnp.bfloat16)
    low = (value - high.astype(jnp.float32)).astype(jnp.bfloat16)
    return high, low


def times(a, b):
    return lax.dot_general(a, b, (((0,), (0,)), ((), ())), preferred_element_type=jnp.float32)


def product(core_ref, rows_ref, own_ref, other_ref, accum_ref, scale_ref, scaled_ref, sums_ref):
    depth = rows_ref.shape[0] * rows_ref.shape[1]
    rows, width = rows_ref.shape[2], own_ref.shape[3]
    high, low = split(rows_ref[...].reshape(depth, rows))
    squares = jnp.zeros((rows, 128), jnp.float32)
    for half in range(2):
        for which in range(CORE):
            mine = core_ref[0] == which
            block = jnp.where(mine, own_ref[:, half], other_ref[:, half]).reshape(depth, width)
            block_high, block_low = split(block)
            part = times(high, block_high) + (times(high, block_low) + times(low, block_high))
            cols = pl.ds((half * CORE + which) * width, width)
            scaled = (accum_ref[:, cols] + part) * scale_ref[:, cols]
            scaled_ref[:, cols] = scaled
            for lane in range(0, width, 128):
                chunk = scaled[:, lane : lane + 128]
                squares += chunk * chunk
    sums = jnp.sum(squares.T, axis=0, keepdims=True)
    sums_ref[...] = jnp.broadcast_to(sums[None], sums_ref.shape)


def divide(scaled_ref, sums_ref, out_ref):
    rows, cols = scaled_ref.shape
    total = jnp.sum(sums_ref[...], axis=0)[:1]
    count = cols * sums_ref.shape[0]
    factor = lax.rsqrt(total / count + 1e-06)
    factor = jnp.broadcast_to(factor, (128, rows)).T
    for lane in range(0, cols, 128):
        out_ref[:, lane : lane + 128] = scaled_ref[:, lane : lane + 128] * factor


def call(kernel, out_shape, inputs, flops=0, scalars=1):
    return pl.pallas_call(
        kernel,
        out_shape=out_shape,
        in_specs=[SMEM] * scalars + [VMEM] * (len(inputs) - scalars),
        out_specs=jax.tree.map(lambda _: VMEM, out_shape),
        compiler_params=pltpu.CompilerParams(vmem_limit_bytes=32 * 1024 * 1024),
        cost_estimate=pl.CostEstimate(flops=flops, bytes_accessed=2 * 1024 * 1024, transcendentals=0),
    )(*inputs)


def f32(*shape):
    return jax.ShapeDtypeStruct(shape, jnp.float32)


def per_device(left_panel, accum, col_scale):
    block = left_panel.T
    depth, rows = block.shape
    cols = accum.shape[1]
    groups = YL * X
    pieces = [lax.ppermute(block, ("yh", "z", "yl"), along_z(shift)) for shift in range(Z)]
    copies = jnp.broadcast_to(block[None], (groups, depth, rows))
    full_rows = lax.all_to_all(copies, COL, 0, 0)

    z = lax.axis_index("z").reshape(1)
    core = lax.axis_index("core").reshape(1)
    planes = call(sort_planes, f32(YH, Z, depth, rows), [z, *pieces])
    planes = planes.reshape(YH * X, Z // X, depth, rows)
    own = lax.all_to_all(planes, ("yh", "x"), 0, 0)
    other = lax.ppermute(own, "core", [(0, 1), (1, 0)])

    scaled, sums = call(
        product,
        (f32(rows, cols), f32(groups, 8, rows)),
        [core, full_rows, own, other, accum, col_scale[None]],
        flops=6 * rows * cols * depth * groups,
    )
    sums = lax.all_to_all(sums, COL, 0, 0)
    return call(divide, f32(rows, cols), [scaled, sums], scalars=0)


def solution(mesh):
    fine = Mesh(mesh.devices.reshape(YH, Z, CORE, YL, X), (*ROW, *COL))
    placed = (P(ROW, COL), P(ROW, COL), P(COL))
    return jax.shard_map(
        per_device, mesh=fine, in_specs=placed, out_specs=P(ROW, COL), check_vma=False
    )
```

time: 226 us -> 77.6 us (0.34)
  waiting for transfers between devices: 160 us -> 18.2 us
  starting transfers between devices: 0.01 us -> 24.8 us
  between operations: 13.4 us -> 0.05 us
  blocking collectives: 41.4 us -> 29 us
  matrix products: 5.3 us -> 0 us
  Pallas kernels: 0 us -> 3.6 us
    all_gather x1 -> x0, waiting for transfers between devices: 160 us -> none  [per_device(): everyone = lax.all_gather(full_rows, 'row', axis=0, tiled=True)]
    all_to_all x0 -> x2, blocking collectives: none -> 29 us  [the longest x1 21.4 us: per_device(): own = lax.all_to_all(planes, ('yh', 'x'), 0, 0)]
    all_gather x1 -> x0, blocking collectives: 26.5 us -> none  [per_device(): full_rows = lax.all_gather(left_panel, 'col', axis=1, tiled=True)]
    ppermute x0 -> x9, starting transfers between devices: none -> 21.3 us  [the longest x8 17.5 us: per_device(): lax.ppermute(block, ('yh', 'z', 'yl'), along_z(shift))]
    psum x1 -> x0, blocking collectives: 14.9 us -> none  [per_device(): totals = lax.psum(jnp.sum(scaled * scaled, axis=1), 'col')]
    all_to_all x0 -> x1, waiting for transfers between devices: none -> 10.3 us  [per_device(): full_rows = lax.all_to_all(copies, COL, 0, 0)]
    ppermute x0 -> x9, waiting for transfers between devices: none -> 7.94 us  [the longest x8 7.93 us: per_device(): lax.ppermute(block, ('yh', 'z', 'yl'), along_z(shift))]
    dot_general x1 -> x0, matrix products: 5.3 us -> none  [per_device(): lax.dot_general(full_rows, mirror, (((1,), (1,)), ((), ())), precision=la...]
  transfers between devices with their start and end apart: 1 -> 10, of which waited for: 1 -> 4; matrix products, arithmetic and copies ran while one was open for 1% -> 1% of each run, Pallas kernels for 0% -> 0%
where the time goes in v1:
time: 77.6 us; the launch traced here: 76.4 us
  blocking collectives  29 us (37%)
  starting transfers between devices  24.8 us (32%)
  waiting for transfers between devices  18.2 us (23%)
  Pallas kernels  3.6 us (5%)
  local copies, waits for them, and re-layouts  0.85 us (1%)
    all_to_all x1, blocking collectives, per_device(): own = lax.all_to_all(planes, ('yh', 'x'), 0, 0)  21.4 us
    ppermute x8, starting transfers between devices, per_device(): lax.ppermute(block, ('yh', 'z', 'yl'), along_z(shift))  17.5 us
    all_to_all x1, waiting for transfers between devices, per_device(): full_rows = lax.all_to_all(copies, COL, 0, 0)  10.3 us
    ppermute x8, waiting for transfers between devices, per_device(): lax.ppermute(block, ('yh', 'z', 'yl'), along_z(shift))  7.93 us
    all_to_all x1, blocking collectives, per_device(): sums = lax.all_to_all(sums, COL, 0, 0)  7.58 us
    ppermute x1, starting transfers between devices, per_device(): other = lax.ppermute(own, 'core', [(0, 1), (1, 0)])  3.76 us
    pallas_call x3, Pallas kernels, call(): pl.pallas_call(kernel, out_shape=out_shape, in_specs=[SMEM] * scalars + [...  3.6 us
    all_to_all x1, starting transfers between devices, per_device(): full_rows = lax.all_to_all(copies, COL, 0, 0)  3.49 us
  transfers between devices with their start and end apart: 10, of which 4 were waited for; matrix products, arithmetic and copies ran while one was open for 1% of the time, Pallas kernels for 0%

profile of v1, /device:TPU:1, one launch (start us, length us, event | category | flops | bytes accessed | tf_op | source)
XLA Modules:
  0.0 76.4 jit_solution(11177761789243428931)
XLA Ops:
  0.0 6.4 %collective-permute-start.7 = (f32[64,256]{1,0:T(8,128)}, f32[64,256]{1,0:T(8,128)S(1)}, u32[]{:S(2)}, u32[]{:S(2)}) collective-permute-start(f32[64,256]{1,0:T(8,128)} %bitcast.7), channel_id=1, source_target_pairs={{0,112},{4,240},{16,0},{20,128},{32,16},{36,144},{48,32},{52,160},... | collective-permute-start | bytes 196616 | tf_op jit(solution)/shard_map/ppermute | solution.py:96
  6.4 1.2 %collective-permute-start.6 = (f32[64,256]{1,0:T(8,128)}, f32[64,256]{1,0:T(8,128)S(1)}, u32[]{:S(2)}, u32[]{:S(2)}) collective-permute-start(f32[64,256]{1,0:T(8,128)} %bitcast.8), channel_id=1, source_target_pairs={{0,96},{4,224},{16,112},{20,240},{32,0},{36,128},{48,16},{52,144},... | collective-permute-start | bytes 196616 | tf_op jit(solution)/shard_map/ppermute | solution.py:96
  7.6 0.4 collective-permute-start.5
  8.0 4.5 %collective-permute-start.4 = (f32[64,256]{1,0:T(8,128)}, f32[64,256]{1,0:T(8,128)S(1)}, u32[]{:S(2)}, u32[]{:S(2)}) collective-permute-start(f32[64,256]{1,0:T(8,128)} %bitcast.10), channel_id=1, source_target_pairs={{0,64},{4,192},{16,80},{20,208},{32,96},{36,224},{48,112},{52,240}... | collective-permute-start | bytes 196616 | tf_op jit(solution)/shard_map/ppermute | solution.py:96
  12.5 0.0 collective-permute-start.3
  12.5 0.0 collective-permute-done.7.refs_7_
  12.5 2.1 %collective-permute-start.2 = (f32[64,256]{1,0:T(8,128)}, f32[64,256]{1,0:T(8,128)S(1)}, u32[]{:S(2)}, u32[]{:S(2)}) collective-permute-start(f32[64,256]{1,0:T(8,128)} %bitcast.12), channel_id=1, source_target_pairs={{0,32},{4,160},{16,48},{20,176},{32,64},{36,192},{48,80},{52,208},... | collective-permute-start | bytes 196616 | tf_op jit(solution)/shard_map/ppermute | solution.py:96
  14.6 0.0 collective-permute-done.6.refs_6_
  14.6 1.5 %collective-permute-start.1 = (f32[64,256]{1,0:T(8,128)}, f32[64,256]{1,0:T(8,128)S(1)}, u32[]{:S(2)}, u32[]{:S(2)}) collective-permute-start(f32[64,256]{1,0:T(8,128)} %bitcast.13), channel_id=1, source_target_pairs={{0,16},{4,144},{16,32},{20,160},{32,48},{36,176},{48,64},{52,192},... | collective-permute-start | bytes 196616 | tf_op jit(solution)/shard_map/ppermute | solution.py:96
  16.1 0.0 collective-permute-done.5.refs_5_
  16.1 1.5 %collective-permute-start = (f32[64,256]{1,0:T(8,128)}, f32[64,256]{1,0:T(8,128)S(1)}, u32[]{:S(2)}, u32[]{:S(2)}) collective-permute-start(f32[64,256]{1,0:T(8,128)} %bitcast.14), channel_id=1, source_target_pairs={{0,0},{4,128},{16,16},{20,144},{32,32},{36,160},{48,48},{52,176},{... | collective-permute-start | bytes 196616 | tf_op jit(solution)/shard_map/ppermute | solution.py:96
  17.5 0.0 collective-permute-done.4.refs_4_
  17.6 1.6 %collective-permute-done.3.refs_3_ = f32[64,256]{1,0:T(8,128)S(1)} collective-permute-done((f32[64,256]{1,0:T(8,128)}, f32[64,256]{1,0:T(8,128)S(1)}, u32[]{:S(2)}, u32[]{:S(2)}) %collective-permute-start.3) | collective-permute-done | bytes 65568 | tf_op jit(solution)/shard_map/ppermute | solution.py:96
  19.2 5.1 %collective-permute-done.2.refs_2_ = f32[64,256]{1,0:T(8,128)S(1)} collective-permute-done((f32[64,256]{1,0:T(8,128)}, f32[64,256]{1,0:T(8,128)S(1)}, u32[]{:S(2)}, u32[]{:S(2)}) %collective-permute-start.2) | collective-permute-done | bytes 65568 | tf_op jit(solution)/shard_map/ppermute | solution.py:96
  24.3 1.2 %collective-permute-done.1.refs_1_ = f32[64,256]{1,0:T(8,128)S(1)} collective-permute-done((f32[64,256]{1,0:T(8,128)}, f32[64,256]{1,0:T(8,128)S(1)}, u32[]{:S(2)}, u32[]{:S(2)}) %collective-permute-start.1) | collective-permute-done | bytes 65568 | tf_op jit(solution)/shard_map/ppermute | solution.py:96
  25.5 0.0 collective-permute-done.refs_0_
  25.5 0.1 shard_map.37
  25.6 0.0 copy-start.2
  25.6 21.4 %all_to_all.15.own_ref = f32[8,2,64,256]{3,2,1,0:T(8,128)S(1)} all-to-all(f32[8,2,64,256]{3,2,1,0:T(8,128)S(1)} %bitcast.5), channel_id=1, replica_groups=mesh['yh'=2,'z'=8,'core'=2,'yl'=2,'x'=4] {'yh','x'}, dimensions={0} | all-to-all | bytes 2097152 | tf_op jit(solution)/shard_map/all_to_all | solution.py:104
  47.0 0.0 copy-start
  47.0 3.8 %collective-permute-start.8 = (f32[8,2,64,256]{3,2,1,0:T(8,128)S(1)}, f32[8,2,64,256]{3,2,1,0:T(8,128)}, u32[]{:S(2)}, u32[]{:S(2)}) collective-permute-start(f32[8,2,64,256]{3,2,1,0:T(8,128)S(1)} %all_to_all.15.own_ref), channel_id=1, source_target_pairs={{0,8},{8,0},{1,9},{9,1},{2,10},{10,2},{3,11},{11,3},{4,12},{12,4},... | collective-permute-start | bytes 3145736 | tf_op jit(solution)/shard_map/ppermute | solution.py:105
  50.7 0.0 copy-done.2
  50.7 0.8 %broadcast_in_dim.4 = f32[8,64,256]{2,1,0:T(8,128)} broadcast(f32[64,256]{1,0:T(8,128)S(1)} %bitcast.15), dimensions={1,2} | broadcast | bytes 589824 | tf_op jit(solution)/shard_map/broadcast_in_dim | solution.py:97
  51.6 3.5 %all-to-all-start = ((f32[8,64,256]{2,1,0:T(8,128)}), f32[8,64,256]{2,1,0:T(8,128)S(1)}, u32[]{:S(2)}, u32[]{:S(2)}) async-start(f32[8,64,256]{2,1,0:T(8,128)} %broadcast_in_dim.4), calls=%async_computation | async-start | bytes 1048576 | tf_op jit(solution)/shard_map/all_to_all | solution.py:98
  55.1 0.0 copy-start.1
  55.1 10.3 %all-to-all-done.rows_ref = f32[8,64,256]{2,1,0:T(8,128)S(1)} async-done(((f32[8,64,256]{2,1,0:T(8,128)}), f32[8,64,256]{2,1,0:T(8,128)S(1)}, u32[]{:S(2)}, u32[]{:S(2)}) %all-to-all-start) | async-done | bytes 524320 | tf_op jit(solution)/shard_map/all_to_all | solution.py:98
  65.3 0.0 collective-permute-done.8.other_ref
  65.3 0.0 copy-done
  65.3 0.0 copy-done.1
  65.3 2.4 %shard_map.38 = (f32[256,1024]{1,0:T(8,128)S(1)}, f32[8,8,256]{2,1,0:T(8,128)S(1)}) custom-call(s32[1]{0:T(128)} %bitcast.core_ref, f32[8,64,256]{2,1,0:T(8,128)S(1)} %all-to-all-done.rows_ref, f32[8,2,64,256]{3,2,1,0:T(8,128)S(1)} %all_to_all.15.own_ref, f32[8,2,64,256]{3,2,1,0:T(8,128)} %collective-permute-done.8.other_ref, f32[256,1024]{1,0:T(8,128)S(1)} %copy-done, ...), custom_call_target="tpu_custom_call" | custom-call | flops 805306368 | bytes 2097152 | tf_op jit(solution)/shard_map/pallas_call | solution.py:77
  67.7 7.6 %all_to_all.16.sums_ref = f32[8,8,256]{2,1,0:T(8,128)S(1)} all-to-all(f32[8,8,256]{2,1,0:T(8,128)S(1)} %get-tuple-element.8), channel_id=1, replica_groups=mesh['yh'=2,'z'=8,'core'=2,'yl'=2,'x'=4] {'yl','x'}, dimensions={0} | all-to-all | bytes 131072 | tf_op jit(solution)/shard_map/all_to_all | solution.py:113
  75.3 1.1 %shard_map.39 = f32[256,1024]{1,0:T(8,128)} custom-call(f32[256,1024]{1,0:T(8,128)S(1)} %get-tuple-element.7.scaled_ref, f32[8,8,256]{2,1,0:T(8,128)S(1)} %all_to_all.16.sums_ref), custom_call_target="tpu_custom_call" | custom-call | bytes 2097152 | tf_op jit(solution)/shard_map/pallas_call | solution.py:77
Async XLA Ops:
  0.0 12.5 %collective-permute-start.7 = (f32[64,256]{1,0:T(8,128)}, f32[64,256]{1,0:T(8,128)S(1)}, u32[]{:S(2)}, u32[]{:S(2)}) collective-permute-start(f32[64,256]{1,0:T(8,128)} %bitcast.7), channel_id=1, source_target_pairs={{0,112},{4,240},{16,0},{20,128},{32,16},{36,144},{48,32},{52,160},... | collective-permute-start | bytes 196616 | tf_op jit(solution)/shard_map/ppermute | solution.py:96
  6.4 8.2 %collective-permute-start.6 = (f32[64,256]{1,0:T(8,128)}, f32[64,256]{1,0:T(8,128)S(1)}, u32[]{:S(2)}, u32[]{:S(2)}) collective-permute-start(f32[64,256]{1,0:T(8,128)} %bitcast.8), channel_id=1, source_target_pairs={{0,96},{4,224},{16,112},{20,240},{32,0},{36,128},{48,16},{52,144},... | collective-permute-start | bytes 196616 | tf_op jit(solution)/shard_map/ppermute | solution.py:96
  7.6 8.5 %collective-permute-start.5 = (f32[64,256]{1,0:T(8,128)}, f32[64,256]{1,0:T(8,128)S(1)}, u32[]{:S(2)}, u32[]{:S(2)}) collective-permute-start(f32[64,256]{1,0:T(8,128)} %bitcast.9), channel_id=1, source_target_pairs={{0,80},{4,208},{16,96},{20,224},{32,112},{36,240},{48,0},{52,128},... | collective-permute-start | bytes 196616 | tf_op jit(solution)/shard_map/ppermute | solution.py:96
  8.0 9.5 %collective-permute-start.4 = (f32[64,256]{1,0:T(8,128)}, f32[64,256]{1,0:T(8,128)S(1)}, u32[]{:S(2)}, u32[]{:S(2)}) collective-permute-start(f32[64,256]{1,0:T(8,128)} %bitcast.10), channel_id=1, source_target_pairs={{0,64},{4,192},{16,80},{20,208},{32,96},{36,224},{48,112},{52,240}... | collective-permute-start | bytes 196616 | tf_op jit(solution)/shard_map/ppermute | solution.py:96
  12.5 6.7 %collective-permute-start.3 = (f32[64,256]{1,0:T(8,128)}, f32[64,256]{1,0:T(8,128)S(1)}, u32[]{:S(2)}, u32[]{:S(2)}) collective-permute-start(f32[64,256]{1,0:T(8,128)} %bitcast.11), channel_id=1, source_target_pairs={{0,48},{4,176},{16,64},{20,192},{32,80},{36,208},{48,96},{52,224},... | collective-permute-start | bytes 196616 | tf_op jit(solution)/shard_map/ppermute | solution.py:96
  12.5 11.8 %collective-permute-start.2 = (f32[64,256]{1,0:T(8,128)}, f32[64,256]{1,0:T(8,128)S(1)}, u32[]{:S(2)}, u32[]{:S(2)}) collective-permute-start(f32[64,256]{1,0:T(8,128)} %bitcast.12), channel_id=1, source_target_pairs={{0,32},{4,160},{16,48},{20,176},{32,64},{36,192},{48,80},{52,208},... | collective-permute-start | bytes 196616 | tf_op jit(solution)/shard_map/ppermute | solution.py:96
  14.6 10.9 %collective-permute-start.1 = (f32[64,256]{1,0:T(8,128)}, f32[64,256]{1,0:T(8,128)S(1)}, u32[]{:S(2)}, u32[]{:S(2)}) collective-permute-start(f32[64,256]{1,0:T(8,128)} %bitcast.13), channel_id=1, source_target_pairs={{0,16},{4,144},{16,32},{20,160},{32,48},{36,176},{48,64},{52,192},... | collective-permute-start | bytes 196616 | tf_op jit(solution)/shard_map/ppermute | solution.py:96
  16.1 9.4 %collective-permute-start = (f32[64,256]{1,0:T(8,128)}, f32[64,256]{1,0:T(8,128)S(1)}, u32[]{:S(2)}, u32[]{:S(2)}) collective-permute-start(f32[64,256]{1,0:T(8,128)} %bitcast.14), channel_id=1, source_target_pairs={{0,0},{4,128},{16,16},{20,144},{32,32},{36,160},{48,48},{52,176},{... | collective-permute-start | bytes 196616 | tf_op jit(solution)/shard_map/ppermute | solution.py:96
  25.6 25.2 %copy-start.2 = (f32[256,64]{0,1:T(8,128)S(1)}, f32[256,64]{0,1:T(8,128)}, u32[]{:S(2)}) copy-start(f32[256,64]{0,1:T(8,128)} %param.3) | copy-start | bytes 196612
  47.0 18.4 %copy-start = (f32[256,1024]{1,0:T(8,128)S(1)}, f32[256,1024]{1,0:T(8,128)}, u32[]{:S(2)}) copy-start(f32[256,1024]{1,0:T(8,128)} %accum_ref.1) | copy-start | bytes 3145732
  47.0 18.4 %collective-permute-start.8 = (f32[8,2,64,256]{3,2,1,0:T(8,128)S(1)}, f32[8,2,64,256]{3,2,1,0:T(8,128)}, u32[]{:S(2)}, u32[]{:S(2)}) collective-permute-start(f32[8,2,64,256]{3,2,1,0:T(8,128)S(1)} %all_to_all.15.own_ref), channel_id=1, source_target_pairs={{0,8},{8,0},{1,9},{9,1},{2,10},{10,2},{3,11},{11,3},{4,12},{12,4},... | collective-permute-start | bytes 3145736 | tf_op jit(solution)/shard_map/ppermute | solution.py:105
  51.6 13.8 %all-to-all-start = ((f32[8,64,256]{2,1,0:T(8,128)}), f32[8,64,256]{2,1,0:T(8,128)S(1)}, u32[]{:S(2)}, u32[]{:S(2)}) async-start(f32[8,64,256]{2,1,0:T(8,128)} %broadcast_in_dim.4), calls=%async_computation | async-start | bytes 1048576 | tf_op jit(solution)/shard_map/all_to_all | solution.py:98
  55.1 10.3 %copy-start.1 = (f32[1024]{0:T(1024)S(1)}, f32[1024]{0:T(1024)}, u32[]{:S(2)}) copy-start(f32[1024]{0:T(1024)} %param.5) | copy-start | bytes 12292

commit v2 on v1

v2 whole, which is shorter than its diff:
```python
import itertools

import jax
import jax.numpy as jnp
from jax import lax
from jax.experimental import pallas as pl
from jax.experimental.pallas import tpu as pltpu
from jax.sharding import Mesh, PartitionSpec as P

YH, Z, CORE, YL, X = SIZES = 2, 8, 2, 2, 4
ROW = ("yh", "z", "core")
COL = ("yl", "x")
ALL = (*ROW, *COL)
NEAR = (1, 2, 3)
VMEM = pl.BlockSpec(memory_space=pltpu.VMEM)
SMEM = pl.BlockSpec(memory_space=pltpu.SMEM)


def send(value, target):
    def index(place):
        found = 0
        for at, size in zip(place, SIZES, strict=True):
            found = found * size + at
        return found

    pairs = [(index(place), index(target(*place))) for place in itertools.product(*map(range, SIZES))]
    return lax.ppermute(value, ALL, pairs)


def across(yh, z, core, yl, x):
    return yh, z, 1 - core, yl, x


def turned(yh, z, core, yl, x):
    return yl, z, core, yh, x


def opposite(yh, z, core, yl, x):
    return yl, (z + Z // 2) % Z, core, yh, x


def along_z(hops):
    def target(yh, z, core, yl, x):
        return yl, (z + (hops if core == 0 else -hops)) % Z, core, yh, x

    return target


def in_plane(step):
    def target(yh, z, core, yl, x):
        return yh ^ core ^ (step // 2), z, core, yl, (x + step) % X

    return target


def sort_planes(place_ref, here_ref, here_beside_ref, far_ref, far_beside_ref, *refs):
    near, near_beside = refs[: len(NEAR)], refs[len(NEAR) : 2 * len(NEAR)]
    outs, sorted_ref = refs[2 * len(NEAR) : -1], refs[-1]
    z, core, x = (place_ref[i] for i in range(3))

    def put(plane, row_core, value):
        plane = lax.rem(plane + 2 * Z, Z)
        sorted_ref[lax.rem(plane // 2 - x + X, X), lax.rem(plane, 2), row_core] = value

    put(z, core, here_ref[...])
    put(z, 1 - core, here_beside_ref[...])
    put(z + Z // 2, core, far_ref[...])
    put(z + Z // 2, 1 - core, far_beside_ref[...])
    for hops, piece, piece_beside in zip(NEAR, near, near_beside, strict=True):
        plane = z + (2 * core - 1) * hops
        plane_beside = z - (2 * core - 1) * hops
        put(plane, core, piece[0])
        put(plane, 1 - core, piece[1])
        put(plane_beside, 1 - core, piece_beside[0])
        put(plane_beside, core, piece_beside[1])
    for step, out in enumerate(outs):
        out[...] = sorted_ref[step]


def split(value):
    high = value.astype(jnp.bfloat16)
    low = (value - high.astype(jnp.float32)).astype(jnp.bfloat16)
    return high, low


def times(a, b):
    return lax.dot_general(a, b, (((0,), (0,)), ((), ())), preferred_element_type=jnp.float32)


def product(place_ref, rows_ref, accum_ref, scale_ref, *refs):
    pieces, (scaled_ref, sums_ref) = refs[: 2 * X], refs[2 * X :]
    yh, core, x = (place_ref[i] for i in range(3))
    ordered = []
    for flip in (core, 1 - core):
        for step in range(X):
            ordered.append(rows_ref[lax.rem(yh + flip + step // 2, 2) * X + lax.rem(x - step + X, X)])
    high, low = split(jnp.concatenate(ordered, axis=0))
    rows, width = rows_ref.shape[2], pieces[0].shape[3]
    squares = jnp.zeros((rows, 128), jnp.float32)
    for odd in range(2):
        for row_core in range(CORE):
            block = jnp.concatenate([piece[odd, row_core] for piece in pieces], axis=0)
            block_high, block_low = split(block)
            part = times(high, block_high) + (times(high, block_low) + times(low, block_high))
            cols = pl.ds((odd * CORE + row_core) * width, width)
            scaled = (accum_ref[:, cols] + part) * scale_ref[:, cols]
            scaled_ref[:, cols] = scaled
            for lane in range(0, width, 128):
                chunk = scaled[:, lane : lane + 128]
                squares += chunk * chunk
    sums = jnp.sum(squares.T, axis=0, keepdims=True)
    sums_ref[...] = jnp.broadcast_to(sums[None], sums_ref.shape)


def divide(scaled_ref, sums_ref, out_ref):
    rows, cols = scaled_ref.shape
    total = jnp.sum(sums_ref[...], axis=0)[:1]
    count = cols * sums_ref.shape[0]
    factor = lax.rsqrt(total / count + 1e-06)
    factor = jnp.broadcast_to(factor, (128, rows)).T
    for lane in range(0, cols, 128):
        out_ref[:, lane : lane + 128] = scaled_ref[:, lane : lane + 128] * factor


def call(kernel, out_shape, inputs, scalars=1, scratch=(), flops=0):
    return pl.pallas_call(
        kernel,
        out_shape=out_shape,
        in_specs=[SMEM] * scalars + [VMEM] * (len(inputs) - scalars),
        out_specs=jax.tree.map(lambda _: VMEM, out_shape),
        scratch_shapes=list(scratch),
        compiler_params=pltpu.CompilerParams(vmem_limit_bytes=16 * 1024 * 1024),
        cost_estimate=pl.CostEstimate(flops=flops, bytes_accessed=2 * 1024 * 1024, transcendentals=0),
    )(*inputs)


def f32(*shape):
    return jax.ShapeDtypeStruct(shape, jnp.float32)


def place(*names):
    return jnp.stack([lax.axis_index(name) for name in names])


def per_device(left_panel, accum, col_scale):
    block = left_panel.T
    depth, rows = block.shape
    cols = accum.shape[1]
    groups = YL * X

    copies = jnp.broadcast_to(block[None], (groups, depth, rows))
    full_rows = lax.all_to_all(copies, COL, 0, 0)
    here = send(block, turned)
    both = jnp.stack([block, send(block, across)])
    near = [send(both, along_z(hops)) for hops in NEAR]
    far = send(block, opposite)
    far_beside = send(far, across)
    here_beside = send(here, across)
    near_beside = [send(piece, across) for piece in near]

    planes = call(
        sort_planes,
        (f32(2, CORE, depth, rows),) * X,
        [place("z", "core", "x"), here, here_beside, far, far_beside, *near, *near_beside],
        scratch=[pltpu.VMEM((X, 2, CORE, depth, rows), jnp.float32)],
    )
    mine = [send(planes[step], in_plane(step)) for step in range(X)]
    others = [send(piece, across) for piece in mine]

    scaled, sums = call(
        product,
        (f32(rows, cols), f32(groups, 8, rows)),
        [place("yh", "core", "x"), full_rows, accum, col_scale[None], *mine, *others],
        flops=6 * rows * cols * depth * groups,
    )
    sums = lax.all_to_all(sums, COL, 0, 0)
    return call(divide, f32(rows, cols), [scaled, sums], scalars=0)


def solution(mesh):
    fine = Mesh(mesh.devices.reshape(SIZES), ALL)
    placed = (P(ROW, COL), P(ROW, COL), P(COL))
    return jax.shard_map(
        per_device, mesh=fine, in_specs=placed, out_specs=P(ROW, COL), check_vma=False
    )
```

time: 77.6 us -> 67.7 us (0.87); the launches traced: 76.4 us -> 67.3 us
  blocking collectives: 29 us -> 10.5 us
  starting transfers between devices: 24.8 us -> 33.7 us
  waiting for transfers between devices: 18.2 us -> 16.4 us
  other arithmetic: 0 us -> 1.07 us
  Pallas kernels: 3.6 us -> 4.65 us
    all_to_all x1 -> x0, blocking collectives: 21.4 us -> none  [per_device(): own = lax.all_to_all(planes, ('yh', 'x'), 0, 0)]
    ppermute x9 -> x19, starting transfers between devices: 21.3 us -> 30.2 us  [send(): return lax.ppermute(value, ALL, pairs)]
    all_to_all x1, waiting for transfers between devices: 10.3 us -> 3.87 us  [per_device(): full_rows = lax.all_to_all(copies, COL, 0, 0)]
    ppermute x9 -> x19, waiting for transfers between devices: 7.94 us -> 12.5 us  [send(): return lax.ppermute(value, ALL, pairs)]
    all_to_all x1, blocking collectives: 7.58 us -> 10.5 us  [per_device(): sums = lax.all_to_all(sums, COL, 0, 0)]
    another operation x0 -> x3, other arithmetic: none -> 1.07 us  [the longest x1 0.92 us: per_device(): both = jnp.stack([block, send(block, across)])]
    pallas_call x3, Pallas kernels: 3.6 us -> 4.65 us  [call(): pl.pallas_call(kernel, out_shape=out_shape, in_specs=[SMEM] * scalars + [...]
  transfers between devices with their start and end apart: 10 -> 20, of which waited for: 4 -> 8; matrix products, arithmetic and copies ran while one was open for 1% -> 1% of each run, Pallas kernels for 0% -> 0%
where the time goes in v2:
time: 67.7 us; the launch traced here: 67.3 us
  starting transfers between devices  33.7 us (50%)
  waiting for transfers between devices  16.4 us (24%)
  blocking collectives  10.5 us (16%)
  Pallas kernels  4.65 us (7%)
  other arithmetic  1.07 us (2%)
  local copies, waits for them, and re-layouts  0.85 us (1%)
    ppermute x19, starting transfers between devices, send(): return lax.ppermute(value, ALL, pairs)  30.2 us
    ppermute x19, waiting for transfers between devices, send(): return lax.ppermute(value, ALL, pairs)  12.5 us
    all_to_all x1, blocking collectives, per_device(): sums = lax.all_to_all(sums, COL, 0, 0)  10.5 us
    pallas_call x3, Pallas kernels, call(): pl.pallas_call(kernel, out_shape=out_shape, in_specs=[SMEM] * scalars + [...  4.65 us
    all_to_all x1, waiting for transfers between devices, per_device(): full_rows = lax.all_to_all(copies, COL, 0, 0)  3.87 us
    all_to_all x1, starting transfers between devices, per_device(): full_rows = lax.all_to_all(copies, COL, 0, 0)  3.49 us
  transfers between devices with their start and end apart: 20, of which 8 were waited for; matrix products, arithmetic and copies ran while one was open for 1% of the time, Pallas kernels for 0%

profile of v2, /device:TPU:1, one launch (start us, length us, event | category | flops | bytes accessed | tf_op | source)
XLA Modules:
  0.0 67.3 jit_solution(2634362457121932605)
XLA Ops:
  0.0 3.2 %collective-permute-start.4 = (f32[64,256]{1,0:T(8,128)}, f32[64,256]{1,0:T(8,128)S(1)}, u32[]{:S(2)}, u32[]{:S(2)}) collective-permute-start(f32[64,256]{1,0:T(8,128)} %bitcast.10), channel_id=1, source_target_pairs={{0,8},{1,9},{2,10},{3,11},{4,12},{5,13},{6,14},{7,15},{8,0},{9,1},... | collective-permute-start | bytes 196616 | tf_op jit(solution)/shard_map/ppermute | solution.py:27
  3.2 1.1 %collective-permute-done.4 = f32[64,256]{1,0:T(8,128)S(1)} collective-permute-done((f32[64,256]{1,0:T(8,128)}, f32[64,256]{1,0:T(8,128)S(1)}, u32[]{:S(2)}, u32[]{:S(2)}) %collective-permute-start.4) | collective-permute-done | bytes 65568 | tf_op jit(solution)/shard_map/ppermute | solution.py:27
  4.4 0.9 %pad_maximum_fusion = f32[2,64,256]{2,1,0:T(8,128)S(1)} fusion(f32[1,64,256]{2,1,0:T(8,128)S(1)} %bitcast.15, f32[1,64,256]{2,1,0:T(8,128)} %bitcast.11), kind=kLoop, calls=%fused_computation | loop fusion | flops 32768 | bytes 262144 | tf_op jit(solution)/shard_map/stack | solution.py:154
  5.3 4.8 %collective-permute-start.7 = (f32[2,64,256]{2,1,0:T(8,128)S(1)}, f32[2,64,256]{2,1,0:T(8,128)S(1)}, u32[]{:S(2)}, u32[]{:S(2)}) collective-permute-start(f32[2,64,256]{2,1,0:T(8,128)S(1)} %pad_maximum_fusion), channel_id=1, source_target_pairs={{0,48},{1,49},{2,50},{3,51},{4,176},{5,177},{6,178},{7,179},{8,88}... | collective-permute-start | bytes 393224 | tf_op jit(solution)/shard_map/ppermute | solution.py:27
  10.1 0.3 collective-permute-start.6
  10.4 0.5 collective-permute-start.5
  10.8 4.5 %collective-permute-start.2 = (f32[64,256]{1,0:T(8,128)S(1)}, f32[64,256]{1,0:T(8,128)S(1)}, u32[]{:S(2)}, u32[]{:S(2)}) collective-permute-start(f32[64,256]{1,0:T(8,128)S(1)} %bitcast.12), channel_id=1, source_target_pairs={{0,64},{1,65},{2,66},{3,67},{4,192},{5,193},{6,194},{7,195},{8,72}... | collective-permute-start | bytes 196616 | tf_op jit(solution)/shard_map/ppermute | solution.py:27
  15.3 0.7 collective-permute-start
  16.0 0.1 collective-permute-start.10
  16.1 2.2 %collective-permute-done.6.refs_1_ = f32[2,64,256]{2,1,0:T(8,128)S(1)} collective-permute-done((f32[2,64,256]{2,1,0:T(8,128)S(1)}, f32[2,64,256]{2,1,0:T(8,128)S(1)}, u32[]{:S(2)}, u32[]{:S(2)}) %collective-permute-start.6) | collective-permute-done | bytes 131104 | tf_op jit(solution)/shard_map/ppermute | solution.py:27
  18.3 1.6 %collective-permute-start.9 = (f32[2,64,256]{2,1,0:T(8,128)S(1)}, f32[2,64,256]{2,1,0:T(8,128)S(1)}, u32[]{:S(2)}, u32[]{:S(2)}) collective-permute-start(f32[2,64,256]{2,1,0:T(8,128)S(1)} %collective-permute-done.6.refs_1_), channel_id=1, source_target_pairs={{0,8},{1,9},{2,10},{3,11},{4,12},{5,13},{6,14},{7,15},{8,0},{9,1},... | collective-permute-start | bytes 393224 | tf_op jit(solution)/shard_map/ppermute | solution.py:27
  20.0 1.9 %collective-permute-done.5.refs_0_ = f32[2,64,256]{2,1,0:T(8,128)S(1)} collective-permute-done((f32[2,64,256]{2,1,0:T(8,128)S(1)}, f32[2,64,256]{2,1,0:T(8,128)S(1)}, u32[]{:S(2)}, u32[]{:S(2)}) %collective-permute-start.5) | collective-permute-done | bytes 131104 | tf_op jit(solution)/shard_map/ppermute | solution.py:27
  21.8 1.3 %collective-permute-start.8 = (f32[2,64,256]{2,1,0:T(8,128)S(1)}, f32[2,64,256]{2,1,0:T(8,128)S(1)}, u32[]{:S(2)}, u32[]{:S(2)}) collective-permute-start(f32[2,64,256]{2,1,0:T(8,128)S(1)} %collective-permute-done.5.refs_0_), channel_id=1, source_target_pairs={{0,8},{1,9},{2,10},{3,11},{4,12},{5,13},{6,14},{7,15},{8,0},{9,1},... | collective-permute-start | bytes 393224 | tf_op jit(solution)/shard_map/ppermute | solution.py:27
  23.1 2.1 %collective-permute-start.3 = (f32[64,256]{1,0:T(8,128)S(1)}, f32[64,256]{1,0:T(8,128)S(1)}, u32[]{:S(2)}, u32[]{:S(2)}) collective-permute-start(f32[64,256]{1,0:T(8,128)S(1)} %collective-permute-done.2.far_ref), channel_id=1, source_target_pairs={{0,8},{1,9},{2,10},{3,11},{4,12},{5,13},{6,14},{7,15},{8,0},{9,1},... | collective-permute-start | bytes 196616 | tf_op jit(solution)/shard_map/ppermute | solution.py:27
  25.2 0.1 add_add_fusion.1.place_ref
  25.3 0.8 %collective-permute-done.3.far_beside_ref = f32[64,256]{1,0:T(8,128)S(1)} collective-permute-done((f32[64,256]{1,0:T(8,128)S(1)}, f32[64,256]{1,0:T(8,128)S(1)}, u32[]{:S(2)}, u32[]{:S(2)}) %collective-permute-start.3) | collective-permute-done | bytes 65568 | tf_op jit(solution)/shard_map/ppermute | solution.py:27
  26.1 0.4 collective-permute-done.1.here_beside_ref
  26.5 1.4 %shard_map.37 = (f32[2,2,64,256]{3,2,1,0:T(8,128)S(1)}, f32[2,2,64,256]{3,2,1,0:T(8,128)S(1)}, f32[2,2,64,256]{3,2,1,0:T(8,128)S(1)}, f32[2,2,64,256]{3,2,1,0:T(8,128)}) custom-call(s32[3]{0:T(128)S(1)} %add_add_fusion.1.place_ref, f32[64,256]{1,0:T(8,128)S(1)} %collective-permute-done.here_ref, f32[64,256]{1,0:T(8,128)S(1)} %collective-permute-done.1.here_beside_ref, ...), custom_call_target="tpu_custom_call" | custom-call | bytes 2097152 | tf_op jit(solution)/shard_map/pallas_call | solution.py:126
  27.9 6.0 %collective-permute-start.11 = (f32[2,2,64,256]{3,2,1,0:T(8,128)S(1)}, f32[2,2,64,256]{3,2,1,0:T(8,128)S(1)}, u32[]{:S(2)}, u32[]{:S(2)}) collective-permute-start(f32[2,2,64,256]{3,2,1,0:T(8,128)S(1)} %get-tuple-element.11), channel_id=1, source_target_pairs={{0,0},{1,1},{2,2},{3,3},{4,4},{5,5},{6,6},{7,7},{8,136},{9,137},{1... | collective-permute-start | bytes 786440 | tf_op jit(solution)/shard_map/ppermute | solution.py:27
  33.9 1.0 %collective-permute-start.12 = (f32[2,2,64,256]{3,2,1,0:T(8,128)S(1)}, f32[2,2,64,256]{3,2,1,0:T(8,128)S(1)}, u32[]{:S(2)}, u32[]{:S(2)}) collective-permute-start(f32[2,2,64,256]{3,2,1,0:T(8,128)S(1)} %get-tuple-element.12), channel_id=1, source_target_pairs={{0,1},{1,2},{2,3},{3,0},{4,5},{5,6},{6,7},{7,4},{8,137},{9,138},{1... | collective-permute-start | bytes 786440 | tf_op jit(solution)/shard_map/ppermute | solution.py:27
  34.9 2.5 %collective-permute-start.13 = (f32[2,2,64,256]{3,2,1,0:T(8,128)S(1)}, f32[2,2,64,256]{3,2,1,0:T(8,128)S(1)}, u32[]{:S(2)}, u32[]{:S(2)}) collective-permute-start(f32[2,2,64,256]{3,2,1,0:T(8,128)S(1)} %get-tuple-element.13), channel_id=1, source_target_pairs={{0,130},{1,131},{2,128},{3,129},{4,134},{5,135},{6,132},{7,133},{8... | collective-permute-start | bytes 786440 | tf_op jit(solution)/shard_map/ppermute | solution.py:27
  37.4 1.2 %collective-permute-start.14 = (f32[2,2,64,256]{3,2,1,0:T(8,128)}, f32[2,2,64,256]{3,2,1,0:T(8,128)S(1)}, u32[]{:S(2)}, u32[]{:S(2)}) collective-permute-start(f32[2,2,64,256]{3,2,1,0:T(8,128)} %get-tuple-element.14), channel_id=1, source_target_pairs={{0,131},{1,128},{2,129},{3,130},{4,135},{5,132},{6,133},{7,134},{8... | collective-permute-start | bytes 786440 | tf_op jit(solution)/shard_map/ppermute | solution.py:27
  38.5 0.8 %broadcast_in_dim.11 = f32[8,64,256]{2,1,0:T(8,128)} broadcast(f32[64,256]{1,0:T(8,128)S(1)} %bitcast.14), dimensions={1,2} | broadcast | bytes 589824 | tf_op jit(solution)/shard_map/broadcast_in_dim | solution.py:151
  39.4 3.5 %all-to-all-start = ((f32[8,64,256]{2,1,0:T(8,128)}), f32[8,64,256]{2,1,0:T(8,128)S(1)}, u32[]{:S(2)}, u32[]{:S(2)}) async-start(f32[8,64,256]{2,1,0:T(8,128)} %broadcast_in_dim.11), calls=%async_computation | async-start | bytes 1048576 | tf_op jit(solution)/shard_map/all_to_all | solution.py:152
  42.9 0.1 collective-permute-start.15
  43.0 4.6 %collective-permute-done.12.refs_1_ = f32[2,2,64,256]{3,2,1,0:T(8,128)S(1)} collective-permute-done((f32[2,2,64,256]{3,2,1,0:T(8,128)S(1)}, f32[2,2,64,256]{3,2,1,0:T(8,128)S(1)}, u32[]{:S(2)}, u32[]{:S(2)}) %collective-permute-start.12) | collective-permute-done | bytes 262176 | tf_op jit(solution)/shard_map/ppermute | solution.py:27
  47.6 0.5 collective-permute-start.17
  48.1 1.5 %collective-permute-done.14.refs_3_ = f32[2,2,64,256]{3,2,1,0:T(8,128)S(1)} collective-permute-done((f32[2,2,64,256]{3,2,1,0:T(8,128)}, f32[2,2,64,256]{3,2,1,0:T(8,128)S(1)}, u32[]{:S(2)}, u32[]{:S(2)}) %collective-permute-start.14) | collective-permute-done | bytes 262176 | tf_op jit(solution)/shard_map/ppermute | solution.py:27
  49.7 3.9 %all-to-all-done.rows_ref = f32[8,64,256]{2,1,0:T(8,128)S(1)} async-done(((f32[8,64,256]{2,1,0:T(8,128)}), f32[8,64,256]{2,1,0:T(8,128)S(1)}, u32[]{:S(2)}, u32[]{:S(2)}) %all-to-all-start) | async-done | bytes 524320 | tf_op jit(solution)/shard_map/all_to_all | solution.py:152
  53.6 2.1 %shard_map.38 = (f32[256,1024]{1,0:T(8,128)S(1)}, f32[8,8,256]{2,1,0:T(8,128)S(1)}) custom-call(s32[3]{0:T(128)S(1)} %add_add_fusion.place_ref, f32[8,64,256]{2,1,0:T(8,128)S(1)} %all-to-all-done.rows_ref, f32[256,1024]{1,0:T(8,128)S(1)} %copy-done, f32[1,1024]{1,0:T(1,128)S(1)} %bitcast.9, f32[2,2,64,256]{3,2,1,0:T(8,128)S(1)} %collective-permute-done.11.refs_0_, ...), custom_call_target="tpu_custom_call" | custom-call | flops 805306368 | bytes 2097152 | tf_op jit(solution)/shard_map/pallas_call | solution.py:126
  55.7 10.5 %all_to_all.10.sums_ref = f32[8,8,256]{2,1,0:T(8,128)S(1)} all-to-all(f32[8,8,256]{2,1,0:T(8,128)S(1)} %get-tuple-element.16), channel_id=1, replica_groups=mesh['yh'=2,'z'=8,'core'=2,'yl'=2,'x'=4] {'yl','x'}, dimensions={0} | all-to-all | bytes 131072 | tf_op jit(solution)/shard_map/all_to_all | solution.py:176
  66.2 1.1 %shard_map.39 = f32[256,1024]{1,0:T(8,128)} custom-call(f32[256,1024]{1,0:T(8,128)S(1)} %get-tuple-element.15.scaled_ref, f32[8,8,256]{2,1,0:T(8,128)S(1)} %all_to_all.10.sums_ref), custom_call_target="tpu_custom_call" | custom-call | bytes 2097152 | tf_op jit(solution)/shard_map/pallas_call | solution.py:126
  (22 shorter events, 0.1 us)
Async XLA Ops:
  0.0 4.4 %collective-permute-start.4 = (f32[64,256]{1,0:T(8,128)}, f32[64,256]{1,0:T(8,128)S(1)}, u32[]{:S(2)}, u32[]{:S(2)}) collective-permute-start(f32[64,256]{1,0:T(8,128)} %bitcast.10), channel_id=1, source_target_pairs={{0,8},{1,9},{2,10},{3,11},{4,12},{5,13},{6,14},{7,15},{8,0},{9,1},... | collective-permute-start | bytes 196616 | tf_op jit(solution)/shard_map/ppermute | solution.py:27
  4.4 6.5 %copy-start.2 = (f32[256,64]{0,1:T(8,128)S(1)}, f32[256,64]{0,1:T(8,128)}, u32[]{:S(2)}) copy-start(f32[256,64]{0,1:T(8,128)} %param.3) | copy-start | bytes 196612
  5.3 10.7 %collective-permute-start.7 = (f32[2,64,256]{2,1,0:T(8,128)S(1)}, f32[2,64,256]{2,1,0:T(8,128)S(1)}, u32[]{:S(2)}, u32[]{:S(2)}) collective-permute-start(f32[2,64,256]{2,1,0:T(8,128)S(1)} %pad_maximum_fusion), channel_id=1, source_target_pairs={{0,48},{1,49},{2,50},{3,51},{4,176},{5,177},{6,178},{7,179},{8,88}... | collective-permute-start | bytes 393224 | tf_op jit(solution)/shard_map/ppermute | solution.py:27
  10.1 8.2 %collective-permute-start.6 = (f32[2,64,256]{2,1,0:T(8,128)S(1)}, f32[2,64,256]{2,1,0:T(8,128)S(1)}, u32[]{:S(2)}, u32[]{:S(2)}) collective-permute-start(f32[2,64,256]{2,1,0:T(8,128)S(1)} %pad_maximum_fusion), channel_id=1, source_target_pairs={{0,32},{1,33},{2,34},{3,35},{4,160},{5,161},{6,162},{7,163},{8,104... | collective-permute-start | bytes 393224 | tf_op jit(solution)/shard_map/ppermute | solution.py:27
  10.4 11.5 %collective-permute-start.5 = (f32[2,64,256]{2,1,0:T(8,128)S(1)}, f32[2,64,256]{2,1,0:T(8,128)S(1)}, u32[]{:S(2)}, u32[]{:S(2)}) collective-permute-start(f32[2,64,256]{2,1,0:T(8,128)S(1)} %pad_maximum_fusion), channel_id=1, source_target_pairs={{0,16},{1,17},{2,18},{3,19},{4,144},{5,145},{6,146},{7,147},{8,120... | collective-permute-start | bytes 393224 | tf_op jit(solution)/shard_map/ppermute | solution.py:27
  10.8 12.3 %collective-permute-start.2 = (f32[64,256]{1,0:T(8,128)S(1)}, f32[64,256]{1,0:T(8,128)S(1)}, u32[]{:S(2)}, u32[]{:S(2)}) collective-permute-start(f32[64,256]{1,0:T(8,128)S(1)} %bitcast.12), channel_id=1, source_target_pairs={{0,64},{1,65},{2,66},{3,67},{4,192},{5,193},{6,194},{7,195},{8,72}... | collective-permute-start | bytes 196616 | tf_op jit(solution)/shard_map/ppermute | solution.py:27
  15.3 9.9 %collective-permute-start = (f32[64,256]{1,0:T(8,128)S(1)}, f32[64,256]{1,0:T(8,128)S(1)}, u32[]{:S(2)}, u32[]{:S(2)}) collective-permute-start(f32[64,256]{1,0:T(8,128)S(1)} %bitcast.13), channel_id=1, source_target_pairs={{0,0},{1,1},{2,2},{3,3},{4,128},{5,129},{6,130},{7,131},{8,8},{9,9... | collective-permute-start | bytes 196616 | tf_op jit(solution)/shard_map/ppermute | solution.py:27
  16.0 10.5 %collective-permute-start.10 = (f32[2,64,256]{2,1,0:T(8,128)S(1)}, f32[2,64,256]{2,1,0:T(8,128)S(1)}, u32[]{:S(2)}, u32[]{:S(2)}) collective-permute-start(f32[2,64,256]{2,1,0:T(8,128)S(1)} %collective-permute-done.7.refs_2_), channel_id=1, source_target_pairs={{0,8},{1,9},{2,10},{3,11},{4,12},{5,13},{6,14},{7,15},{8,0},{9,1},... | collective-permute-start | bytes 393224 | tf_op jit(solution)/shard_map/ppermute | solution.py:27
  18.3 8.2 %collective-permute-start.9 = (f32[2,64,256]{2,1,0:T(8,128)S(1)}, f32[2,64,256]{2,1,0:T(8,128)S(1)}, u32[]{:S(2)}, u32[]{:S(2)}) collective-permute-start(f32[2,64,256]{2,1,0:T(8,128)S(1)} %collective-permute-done.6.refs_1_), channel_id=1, source_target_pairs={{0,8},{1,9},{2,10},{3,11},{4,12},{5,13},{6,14},{7,15},{8,0},{9,1},... | collective-permute-start | bytes 393224 | tf_op jit(solution)/shard_map/ppermute | solution.py:27
  21.8 4.6 %collective-permute-start.8 = (f32[2,64,256]{2,1,0:T(8,128)S(1)}, f32[2,64,256]{2,1,0:T(8,128)S(1)}, u32[]{:S(2)}, u32[]{:S(2)}) collective-permute-start(f32[2,64,256]{2,1,0:T(8,128)S(1)} %collective-permute-done.5.refs_0_), channel_id=1, source_target_pairs={{0,8},{1,9},{2,10},{3,11},{4,12},{5,13},{6,14},{7,15},{8,0},{9,1},... | collective-permute-start | bytes 393224 | tf_op jit(solution)/shard_map/ppermute | solution.py:27
  23.1 3.0 %collective-permute-start.3 = (f32[64,256]{1,0:T(8,128)S(1)}, f32[64,256]{1,0:T(8,128)S(1)}, u32[]{:S(2)}, u32[]{:S(2)}) collective-permute-start(f32[64,256]{1,0:T(8,128)S(1)} %collective-permute-done.2.far_ref), channel_id=1, source_target_pairs={{0,8},{1,9},{2,10},{3,11},{4,12},{5,13},{6,14},{7,15},{8,0},{9,1},... | collective-permute-start | bytes 196616 | tf_op jit(solution)/shard_map/ppermute | solution.py:27
  25.2 1.3 %collective-permute-start.1 = (f32[64,256]{1,0:T(8,128)S(1)}, f32[64,256]{1,0:T(8,128)S(1)}, u32[]{:S(2)}, u32[]{:S(2)}) collective-permute-start(f32[64,256]{1,0:T(8,128)S(1)} %collective-permute-done.here_ref), channel_id=1, source_target_pairs={{0,8},{1,9},{2,10},{3,11},{4,12},{5,13},{6,14},{7,15},{8,0},{9,1},... | collective-permute-start | bytes 196616 | tf_op jit(solution)/shard_map/ppermute | solution.py:27
  27.9 25.7 %copy-start = (f32[256,1024]{1,0:T(8,128)S(1)}, f32[256,1024]{1,0:T(8,128)}, u32[]{:S(2)}) copy-start(f32[256,1024]{1,0:T(8,128)} %accum_ref.1) | copy-start | bytes 3145732
  27.9 15.0 %collective-permute-start.11 = (f32[2,2,64,256]{3,2,1,0:T(8,128)S(1)}, f32[2,2,64,256]{3,2,1,0:T(8,128)S(1)}, u32[]{:S(2)}, u32[]{:S(2)}) collective-permute-start(f32[2,2,64,256]{3,2,1,0:T(8,128)S(1)} %get-tuple-element.11), channel_id=1, source_target_pairs={{0,0},{1,1},{2,2},{3,3},{4,4},{5,5},{6,6},{7,7},{8,136},{9,137},{1... | collective-permute-start | bytes 786440 | tf_op jit(solution)/shard_map/ppermute | solution.py:27
  33.9 13.7 %collective-permute-start.12 = (f32[2,2,64,256]{3,2,1,0:T(8,128)S(1)}, f32[2,2,64,256]{3,2,1,0:T(8,128)S(1)}, u32[]{:S(2)}, u32[]{:S(2)}) collective-permute-start(f32[2,2,64,256]{3,2,1,0:T(8,128)S(1)} %get-tuple-element.12), channel_id=1, source_target_pairs={{0,1},{1,2},{2,3},{3,0},{4,5},{5,6},{6,7},{7,4},{8,137},{9,138},{1... | collective-permute-start | bytes 786440 | tf_op jit(solution)/shard_map/ppermute | solution.py:27
  34.9 12.6 %collective-permute-start.13 = (f32[2,2,64,256]{3,2,1,0:T(8,128)S(1)}, f32[2,2,64,256]{3,2,1,0:T(8,128)S(1)}, u32[]{:S(2)}, u32[]{:S(2)}) collective-permute-start(f32[2,2,64,256]{3,2,1,0:T(8,128)S(1)} %get-tuple-element.13), channel_id=1, source_target_pairs={{0,130},{1,131},{2,128},{3,129},{4,134},{5,135},{6,132},{7,133},{8... | collective-permute-start | bytes 786440 | tf_op jit(solution)/shard_map/ppermute | solution.py:27
  37.4 12.2 %collective-permute-start.14 = (f32[2,2,64,256]{3,2,1,0:T(8,128)}, f32[2,2,64,256]{3,2,1,0:T(8,128)S(1)}, u32[]{:S(2)}, u32[]{:S(2)}) collective-permute-start(f32[2,2,64,256]{3,2,1,0:T(8,128)} %get-tuple-element.14), channel_id=1, source_target_pairs={{0,131},{1,128},{2,129},{3,130},{4,135},{5,132},{6,133},{7,134},{8... | collective-permute-start | bytes 786440 | tf_op jit(solution)/shard_map/ppermute | solution.py:27
  39.4 14.2 %all-to-all-start = ((f32[8,64,256]{2,1,0:T(8,128)}), f32[8,64,256]{2,1,0:T(8,128)S(1)}, u32[]{:S(2)}, u32[]{:S(2)}) async-start(f32[8,64,256]{2,1,0:T(8,128)} %broadcast_in_dim.11), calls=%async_computation | async-start | bytes 1048576 | tf_op jit(solution)/shard_map/all_to_all | solution.py:152
  42.9 10.7 %collective-permute-start.15 = (f32[2,2,64,256]{3,2,1,0:T(8,128)S(1)}, f32[2,2,64,256]{3,2,1,0:T(8,128)S(1)}, u32[]{:S(2)}, u32[]{:S(2)}) collective-permute-start(f32[2,2,64,256]{3,2,1,0:T(8,128)S(1)} %collective-permute-done.11.refs_0_), channel_id=1, source_target_pairs={{0,8},{1,9},{2,10},{3,11},{4,12},{5,13},{6,14},{7,15},{8,0},{9,1},... | collective-permute-start | bytes 786440 | tf_op jit(solution)/shard_map/ppermute | solution.py:27
  47.6 6.0 %collective-permute-start.16 = (f32[2,2,64,256]{3,2,1,0:T(8,128)S(1)}, f32[2,2,64,256]{3,2,1,0:T(8,128)S(1)}, u32[]{:S(2)}, u32[]{:S(2)}) collective-permute-start(f32[2,2,64,256]{3,2,1,0:T(8,128)S(1)} %collective-permute-done.12.refs_1_), channel_id=1, source_target_pairs={{0,8},{1,9},{2,10},{3,11},{4,12},{5,13},{6,14},{7,15},{8,0},{9,1},... | collective-permute-start | bytes 786440 | tf_op jit(solution)/shard_map/ppermute | solution.py:27
  47.6 6.0 %collective-permute-start.17 = (f32[2,2,64,256]{3,2,1,0:T(8,128)S(1)}, f32[2,2,64,256]{3,2,1,0:T(8,128)S(1)}, u32[]{:S(2)}, u32[]{:S(2)}) collective-permute-start(f32[2,2,64,256]{3,2,1,0:T(8,128)S(1)} %collective-permute-done.13.refs_2_), channel_id=1, source_target_pairs={{0,8},{1,9},{2,10},{3,11},{4,12},{5,13},{6,14},{7,15},{8,0},{9,1},... | collective-permute-start | bytes 786440 | tf_op jit(solution)/shard_map/ppermute | solution.py:27
  49.6 4.0 %collective-permute-start.18 = (f32[2,2,64,256]{3,2,1,0:T(8,128)S(1)}, f32[2,2,64,256]{3,2,1,0:T(8,128)}, u32[]{:S(2)}, u32[]{:S(2)}) collective-permute-start(f32[2,2,64,256]{3,2,1,0:T(8,128)S(1)} %collective-permute-done.14.refs_3_), channel_id=1, source_target_pairs={{0,8},{1,9},{2,10},{3,11},{4,12},{5,13},{6,14},{7,15},{8,0},{9,1},... | collective-permute-start | bytes 786440 | tf_op jit(solution)/shard_map/ppermute | solution.py:27
  49.6 4.0 %copy-start.1 = (f32[1024]{0:T(1024)S(1)}, f32[1024]{0:T(1024)}, u32[]{:S(2)}) copy-start(f32[1024]{0:T(1024)} %param.5) | copy-start | bytes 12292

commit v3 on v2

v3 whole, which is shorter than its diff:
```python
import itertools

import jax
import jax.numpy as jnp
from jax import lax
from jax.experimental import pallas as pl
from jax.experimental.pallas import tpu as pltpu
from jax.sharding import Mesh, PartitionSpec as P

YH, Z, CORE, YL, X = SIZES = 2, 8, 2, 2, 4
ROW = ("yh", "z", "core")
COL = ("yl", "x")
ALL = (*ROW, *COL)
VMEM = pl.BlockSpec(memory_space=pltpu.VMEM)
SMEM = pl.BlockSpec(memory_space=pltpu.SMEM)


def send(value, target):
    def index(place):
        found = 0
        for at, size in zip(place, SIZES, strict=True):
            found = found * size + at
        return found

    pairs = [(index(place), index(target(*place))) for place in itertools.product(*map(range, SIZES))]
    return lax.ppermute(value, ALL, pairs)


def across(yh, z, core, yl, x):
    return yh, z, 1 - core, yl, x


def turned(yh, z, core, yl, x):
    return yl, z, core, yh, x


def opposite(yh, z, core, yl, x):
    return yl, (z + Z // 2) % Z, core, yh, x


def along_z(hops):
    def target(yh, z, core, yl, x):
        return yl, (z + (hops if core == 0 else -hops)) % Z, core, yh, x

    return target


def pass_on(yh, z, core, yl, x):
    return yh, (z + (1 if core == 0 else -1)) % Z, core, yl, x


def along_x(hops):
    def target(yh, z, core, yl, x):
        return yh, z, core, yl, (x + (hops if core == 0 else -hops)) % X

    return target


def along_y(yh, z, core, yl, x):
    return 1 - yh, z, core, yl, x


def along_yl(yh, z, core, yl, x):
    return yh, z, core, 1 - yl, x


def sort_planes(place_ref, here_ref, here_beside_ref, far_ref, far_beside_ref, near_ref, near_beside_ref, stay_ref, next_ref, second_ref, sorted_ref):
    z, core, x = (place_ref[i] for i in range(3))
    turn = 2 * core - 1

    def put(pair_hops, row_core, value):
        sorted_ref[lax.rem(z // 2 + pair_hops - x + 2 * X, X), row_core] = value

    put(0, core, here_ref[...])
    put(0, 1 - core, here_beside_ref[...])
    put(X // 2, core, far_ref[...])
    put(X // 2, 1 - core, far_beside_ref[...])
    put(turn, core, near_ref[0])
    put(turn, 1 - core, near_ref[1])
    put(-turn, 1 - core, near_beside_ref[0])
    put(-turn, core, near_beside_ref[1])
    stay_ref[...] = sorted_ref[0, core]
    next_ref[...] = sorted_ref[1 + 2 * core]
    second_ref[...] = sorted_ref[X // 2, core]


def split(value):
    high = value.astype(jnp.bfloat16)
    low = (value - high.astype(jnp.float32)).astype(jnp.bfloat16)
    return high, low


def times(a, b):
    return lax.dot_general(a, b, (((0,), (0,)), ((), ())), preferred_element_type=jnp.float32)


def product(place_ref, rows_ref, rows_yl_ref, rows_beside_ref, rows_yl_beside_ref, accum_ref, scale_ref, *refs):
    mine, others, (scaled_ref, sums_ref) = refs[:4], refs[4:8], refs[8:]
    yh, z, core, yl = (place_ref[i] for i in range(4))
    def rows_of(own, beside):
        return [own[0], own[1], beside[2], own[3]]

    here, there = rows_of(rows_ref, rows_beside_ref), rows_of(rows_yl_ref, rows_yl_beside_ref)
    first = [jnp.where(yh == yl, a, b) for a, b in zip(here, there, strict=True)]
    second = [jnp.where(yh == yl, b, a) for a, b in zip(here, there, strict=True)]
    high, low = split(jnp.concatenate(first + second, axis=0))

    def blocks_of(pack, beside):
        one, two = mine[pack], others[pack]
        near, row_core = (one, two)[beside], lax.rem(core + beside, CORE)
        return [near[0], one[1 + row_core], two[1 + row_core], near[3]]

    rows, width = rows_ref.shape[2], refs[0].shape[2]
    squares = jnp.zeros((rows, 128), jnp.float32)
    for odd in range(2):
        for beside in range(CORE):
            block = jnp.concatenate(blocks_of(2 * odd, beside) + blocks_of(2 * odd + 1, beside), axis=0)
            block_high, block_low = split(block)
            part = times(high, block_high) + (times(high, block_low) + times(low, block_high))
            tile = lax.rem(z + odd, 2) * CORE + lax.rem(core + beside, CORE)
            cols = pl.ds(pl.multiple_of(tile * width, width), width)
            scaled = (accum_ref[:, cols] + part) * scale_ref[:, cols]
            scaled_ref[:, cols] = scaled
            for lane in range(0, width, 128):
                chunk = scaled[:, lane : lane + 128]
                squares += chunk * chunk
    sums = jnp.sum(squares.T, axis=0, keepdims=True)
    sums_ref[...] = jnp.broadcast_to(sums[None], sums_ref.shape)


def divide(scaled_ref, sums_ref, out_ref):
    rows, cols = scaled_ref.shape
    total = jnp.sum(sums_ref[...], axis=0)[:1]
    count = cols * sums_ref.shape[0]
    factor = lax.rsqrt(total / count + 1e-06)
    factor = jnp.broadcast_to(factor, (128, rows)).T
    for lane in range(0, cols, 128):
        out_ref[:, lane : lane + 128] = scaled_ref[:, lane : lane + 128] * factor


def call(kernel, out_shape, inputs, scalars=1, scratch=(), flops=0):
    return pl.pallas_call(
        kernel,
        out_shape=out_shape,
        in_specs=[SMEM] * scalars + [VMEM] * (len(inputs) - scalars),
        out_specs=jax.tree.map(lambda _: VMEM, out_shape),
        scratch_shapes=list(scratch),
        compiler_params=pltpu.CompilerParams(vmem_limit_bytes=16 * 1024 * 1024),
        cost_estimate=pl.CostEstimate(flops=flops, bytes_accessed=2 * 1024 * 1024, transcendentals=0),
    )(*inputs)


def f32(*shape):
    return jax.ShapeDtypeStruct(shape, jnp.float32)


def place(*names):
    return jnp.stack([lax.axis_index(name) for name in names])


def per_device(left_panel, accum, col_scale):
    block = left_panel.T
    depth, rows = block.shape
    cols = accum.shape[1]
    groups = YL * X

    here = send(block, turned)
    both = jnp.stack([block, send(block, across)])
    near = send(both, along_z(2))
    rows_next = send(both, along_x(1))
    rows_second = send(block, along_x(X // 2))
    far = send(block, opposite)
    here_beside, far_beside, near_beside = (send(piece, across) for piece in (here, far, near))

    stay, to_next, to_second = call(
        sort_planes,
        (f32(depth, rows), f32(CORE, depth, rows), f32(depth, rows)),
        [place("z", "core", "x"), here, here_beside, far, far_beside, near, near_beside],
        scratch=[pltpu.VMEM((X, CORE, depth, rows), jnp.float32)],
    )
    from_next = send(to_next, along_x(1))
    from_second = send(to_second, along_x(X // 2))
    kept = jnp.concatenate([stay[None], from_next, from_second[None]])
    other_y = send(kept, along_y)
    other_y, rows_next, rows_second = lax.optimization_barrier((other_y, rows_next, rows_second))
    pack = jnp.concatenate([block[None], rows_next, rows_second[None]])
    full_rows = [pack, send(pack, along_yl)]
    full_rows += [send(part, across) for part in full_rows]
    mine = [kept, other_y, send(kept, pass_on), send(other_y, pass_on)]
    others = [send(pack, across) for pack in mine]

    scaled, sums = call(
        product,
        (f32(rows, cols), f32(groups, 8, rows)),
        [place("yh", "z", "core", "yl"), *full_rows, accum, col_scale[None], *mine, *others],
        flops=6 * rows * cols * depth * groups,
    )
    sums = lax.all_to_all(sums, COL, 0, 0)
    return call(divide, f32(rows, cols), [scaled, sums], scalars=0)


def solution(mesh):
    fine = Mesh(mesh.devices.reshape(SIZES), ALL)
    placed = (P(ROW, COL), P(ROW, COL), P(COL))
    return jax.shard_map(
        per_device, mesh=fine, in_specs=placed, out_specs=P(ROW, COL), check_vma=False
    )
```

time: 67.7 us -> 63 us (0.931)
  blocking collectives: 10.5 us -> 8.59 us
  starting transfers between devices: 33.7 us -> 32.4 us
  local copies, waits for them, and re-layouts: 0.85 us -> 0.01 us
    ppermute x19 -> x21, waiting for transfers between devices: 12.5 us -> 16.6 us  [send(): return lax.ppermute(value, ALL, pairs)]
    all_to_all x1 -> x0, waiting for transfers between devices: 3.87 us -> none  [per_device(): full_rows = lax.all_to_all(copies, COL, 0, 0)]
    all_to_all x1 -> x0, starting transfers between devices: 3.49 us -> none  [per_device(): full_rows = lax.all_to_all(copies, COL, 0, 0)]
    ppermute x19 -> x21, starting transfers between devices: 30.2 us -> 32.4 us  [send(): return lax.ppermute(value, ALL, pairs)]
    all_to_all x1, blocking collectives: 10.5 us -> 8.59 us  [per_device(): sums = lax.all_to_all(sums, COL, 0, 0)]
    broadcast_in_dim x1 -> x0, local copies, waits for them, and re-layouts: 0.84 us -> none  [per_device(): copies = jnp.broadcast_to(block[None], (groups, depth, rows))]
  transfers between devices with their start and end apart: 20 -> 21, of which waited for: 8 -> 9; matrix products, arithmetic and copies ran while one was open for 1% -> 0% of each run, Pallas kernels for 0% -> 0%
where the time goes in v3:
time: 63 us; the launch traced here: 62.7 us
  starting transfers between devices  32.4 us (51%)
  waiting for transfers between devices  16.6 us (26%)
  blocking collectives  8.59 us (14%)
  Pallas kernels  4 us (6%)
  other arithmetic  1.04 us (2%)
    ppermute x21, starting transfers between devices, send(): return lax.ppermute(value, ALL, pairs)  32.4 us
    ppermute x21, waiting for transfers between devices, send(): return lax.ppermute(value, ALL, pairs)  16.6 us
    all_to_all x1, blocking collectives, per_device(): sums = lax.all_to_all(sums, COL, 0, 0)  8.59 us
    pallas_call x3, Pallas kernels, call(): pl.pallas_call(kernel, out_shape=out_shape, in_specs=[SMEM] * scalars + [...  4 us
  transfers between devices with their start and end apart: 21, of which 9 were waited for; matrix products, arithmetic and copies ran while one was open for 0% of the time, Pallas kernels for 0%

profile of v3, /device:TPU:1, one launch (start us, length us, event | category | flops | bytes accessed | tf_op | source)
XLA Modules:
  0.0 62.7 jit_solution(13276456372910423946)
XLA Ops:
  0.0 3.2 %collective-permute-start.4 = (f32[64,256]{1,0:T(8,128)}, f32[64,256]{1,0:T(8,128)S(1)}, u32[]{:S(2)}, u32[]{:S(2)}) collective-permute-start(f32[64,256]{1,0:T(8,128)} %bitcast.15), channel_id=1, source_target_pairs={{0,8},{1,9},{2,10},{3,11},{4,12},{5,13},{6,14},{7,15},{8,0},{9,1},... | collective-permute-start | bytes 196616 | tf_op jit(solution)/shard_map/ppermute | solution.py:26
  3.2 1.1 %collective-permute-done.4 = f32[64,256]{1,0:T(8,128)S(1)} collective-permute-done((f32[64,256]{1,0:T(8,128)}, f32[64,256]{1,0:T(8,128)S(1)}, u32[]{:S(2)}, u32[]{:S(2)}) %collective-permute-start.4) | collective-permute-done | bytes 65568 | tf_op jit(solution)/shard_map/ppermute | solution.py:26
  4.4 0.8 %pad_maximum_fusion.2 = f32[2,64,256]{2,1,0:T(8,128)S(1)} fusion(f32[1,64,256]{2,1,0:T(8,128)S(1)} %bitcast.21, f32[1,64,256]{2,1,0:T(8,128)} %bitcast.16), kind=kLoop, calls=%fused_computation.2 | loop fusion | flops 32768 | bytes 262144 | tf_op jit(solution)/shard_map/stack | solution.py:168
  5.2 4.4 %collective-permute-start.5 = (f32[2,64,256]{2,1,0:T(8,128)S(1)}, f32[2,64,256]{2,1,0:T(8,128)S(1)}, u32[]{:S(2)}, u32[]{:S(2)}) collective-permute-start(f32[2,64,256]{2,1,0:T(8,128)S(1)} %pad_maximum_fusion.2), channel_id=1, source_target_pairs={{0,32},{1,33},{2,34},{3,35},{4,160},{5,161},{6,162},{7,163},{8,104... | collective-permute-start | bytes 393224 | tf_op jit(solution)/shard_map/ppermute | solution.py:26
  9.6 1.0 %collective-permute-start.2 = (f32[64,256]{1,0:T(8,128)}, f32[64,256]{1,0:T(8,128)S(1)}, u32[]{:S(2)}, u32[]{:S(2)}) collective-permute-start(f32[64,256]{1,0:T(8,128)} %bitcast.17), channel_id=1, source_target_pairs={{0,64},{1,65},{2,66},{3,67},{4,192},{5,193},{6,194},{7,195},{8,72}... | collective-permute-start | bytes 196616 | tf_op jit(solution)/shard_map/ppermute | solution.py:26
  10.6 1.5 %collective-permute-start = (f32[64,256]{1,0:T(8,128)}, f32[64,256]{1,0:T(8,128)S(1)}, u32[]{:S(2)}, u32[]{:S(2)}) collective-permute-start(f32[64,256]{1,0:T(8,128)} %bitcast.18), channel_id=1, source_target_pairs={{0,0},{1,1},{2,2},{3,3},{4,128},{5,129},{6,130},{7,131},{8,8},{9,9... | collective-permute-start | bytes 196616 | tf_op jit(solution)/shard_map/ppermute | solution.py:26
  12.0 1.5 %collective-permute-done.5.near_ref = f32[2,64,256]{2,1,0:T(8,128)S(1)} collective-permute-done((f32[2,64,256]{2,1,0:T(8,128)S(1)}, f32[2,64,256]{2,1,0:T(8,128)S(1)}, u32[]{:S(2)}, u32[]{:S(2)}) %collective-permute-start.5) | collective-permute-done | bytes 131104 | tf_op jit(solution)/shard_map/ppermute | solution.py:26
  13.6 0.5 collective-permute-start.6
  14.1 3.5 %collective-permute-done.2.far_ref = f32[64,256]{1,0:T(8,128)S(1)} collective-permute-done((f32[64,256]{1,0:T(8,128)}, f32[64,256]{1,0:T(8,128)S(1)}, u32[]{:S(2)}, u32[]{:S(2)}) %collective-permute-start.2) | collective-permute-done | bytes 65568 | tf_op jit(solution)/shard_map/ppermute | solution.py:26
  17.6 0.3 collective-permute-start.3
  18.2 0.7 %collective-permute-done.3.far_beside_ref = f32[64,256]{1,0:T(8,128)S(1)} collective-permute-done((f32[64,256]{1,0:T(8,128)S(1)}, f32[64,256]{1,0:T(8,128)S(1)}, u32[]{:S(2)}, u32[]{:S(2)}) %collective-permute-start.3) | collective-permute-done | bytes 65568 | tf_op jit(solution)/shard_map/ppermute | solution.py:26
  18.9 0.3 collective-permute-done.1.here_beside_ref
  19.2 0.6 shard_map.37
  19.8 2.6 %collective-permute-start.7 = (f32[2,64,256]{2,1,0:T(8,128)S(1)}, f32[2,64,256]{2,1,0:T(8,128)S(1)}, u32[]{:S(2)}, u32[]{:S(2)}) collective-permute-start(f32[2,64,256]{2,1,0:T(8,128)S(1)} %get-tuple-element.14), channel_id=1, source_target_pairs={{0,1},{1,2},{2,3},{3,0},{4,5},{5,6},{6,7},{7,4},{8,11},{9,8},{10,9... | collective-permute-start | bytes 393224 | tf_op jit(solution)/shard_map/ppermute | solution.py:26
  22.3 0.5 collective-permute-start.8
  22.9 5.1 %collective-permute-done.8 = f32[64,256]{1,0:T(8,128)S(1)} collective-permute-done((f32[64,256]{1,0:T(8,128)S(1)}, f32[64,256]{1,0:T(8,128)S(1)}, u32[]{:S(2)}, u32[]{:S(2)}) %collective-permute-start.8) | collective-permute-done | bytes 65568 | tf_op jit(solution)/shard_map/ppermute | solution.py:26
  28.0 4.7 %collective-permute-start.9 = (f32[4,64,256]{2,1,0:T(8,128)S(1)}, f32[4,64,256]{2,1,0:T(8,128)S(1)}, u32[]{:S(2)}, u32[]{:S(2)}) collective-permute-start(f32[4,64,256]{2,1,0:T(8,128)S(1)} %pad_maximum_fusion.refs_0_), channel_id=1, source_target_pairs={{0,128},{1,129},{2,130},{3,131},{4,132},{5,133},{6,134},{7,135},{8... | collective-permute-start | bytes 786440 | tf_op jit(solution)/shard_map/ppermute | solution.py:26
  32.7 0.8 %collective-permute-start.10 = (f32[2,64,256]{2,1,0:T(8,128)S(1)}, f32[2,64,256]{2,1,0:T(8,128)S(1)}, u32[]{:S(2)}, u32[]{:S(2)}) collective-permute-start(f32[2,64,256]{2,1,0:T(8,128)S(1)} %pad_maximum_fusion.2), channel_id=1, source_target_pairs={{0,1},{1,2},{2,3},{3,0},{4,5},{5,6},{6,7},{7,4},{8,11},{9,8},{10,9... | collective-permute-start | bytes 393224 | tf_op jit(solution)/shard_map/ppermute | solution.py:26
  33.6 2.3 %collective-permute-start.17 = (f32[4,64,256]{2,1,0:T(8,128)S(1)}, f32[4,64,256]{2,1,0:T(8,128)S(1)}, u32[]{:S(2)}, u32[]{:S(2)}) collective-permute-start(f32[4,64,256]{2,1,0:T(8,128)S(1)} %pad_maximum_fusion.refs_0_), channel_id=1, source_target_pairs={{0,8},{1,9},{2,10},{3,11},{4,12},{5,13},{6,14},{7,15},{8,0},{9,1},... | collective-permute-start | bytes 786440 | tf_op jit(solution)/shard_map/ppermute | solution.py:26
  35.8 1.7 %collective-permute-start.15 = (f32[4,64,256]{2,1,0:T(8,128)S(1)}, f32[4,64,256]{2,1,0:T(8,128)S(1)}, u32[]{:S(2)}, u32[]{:S(2)}) collective-permute-start(f32[4,64,256]{2,1,0:T(8,128)S(1)} %pad_maximum_fusion.refs_0_), channel_id=1, source_target_pairs={{0,16},{1,17},{2,18},{3,19},{4,20},{5,21},{6,22},{7,23},{8,120},{9... | collective-permute-start | bytes 786440 | tf_op jit(solution)/shard_map/ppermute | solution.py:26
  37.6 1.6 %collective-permute-done.11 = f32[64,256]{1,0:T(8,128)S(1)} collective-permute-done((f32[64,256]{1,0:T(8,128)S(1)}, f32[64,256]{1,0:T(8,128)S(1)}, u32[]{:S(2)}, u32[]{:S(2)}) %collective-permute-start.11) | collective-permute-done | bytes 65568 | tf_op jit(solution)/shard_map/ppermute | solution.py:26
  39.2 0.7 %collective-permute-start.12 = (f32[4,64,256]{2,1,0:T(8,128)S(1)}, f32[4,64,256]{2,1,0:T(8,128)S(1)}, u32[]{:S(2)}, u32[]{:S(2)}) collective-permute-start(f32[4,64,256]{2,1,0:T(8,128)S(1)} %pad_maximum_fusion.1.rows_ref), channel_id=1, source_target_pairs={{0,4},{1,5},{2,6},{3,7},{4,0},{5,1},{6,2},{7,3},{8,12},{9,13},{10,... | collective-permute-start | bytes 786440 | tf_op jit(solution)/shard_map/ppermute | solution.py:26
  39.8 1.6 %collective-permute-start.16 = (f32[4,64,256]{2,1,0:T(8,128)S(1)}, f32[4,64,256]{2,1,0:T(8,128)S(1)}, u32[]{:S(2)}, u32[]{:S(2)}) collective-permute-start(f32[4,64,256]{2,1,0:T(8,128)S(1)} %collective-permute-done.9.refs_1_), channel_id=1, source_target_pairs={{0,16},{1,17},{2,18},{3,19},{4,20},{5,21},{6,22},{7,23},{8,120},{9... | collective-permute-start | bytes 786440 | tf_op jit(solution)/shard_map/ppermute | solution.py:26
  41.5 1.5 %collective-permute-start.13 = (f32[4,64,256]{2,1,0:T(8,128)S(1)}, f32[4,64,256]{2,1,0:T(8,128)S(1)}, u32[]{:S(2)}, u32[]{:S(2)}) collective-permute-start(f32[4,64,256]{2,1,0:T(8,128)S(1)} %pad_maximum_fusion.1.rows_ref), channel_id=1, source_target_pairs={{0,8},{1,9},{2,10},{3,11},{4,12},{5,13},{6,14},{7,15},{8,0},{9,1},... | collective-permute-start | bytes 786440 | tf_op jit(solution)/shard_map/ppermute | solution.py:26
  43.0 0.5 collective-permute-start.19
  43.5 1.5 %collective-permute-done.12.rows_yl_ref = f32[4,64,256]{2,1,0:T(8,128)S(1)} collective-permute-done((f32[4,64,256]{2,1,0:T(8,128)S(1)}, f32[4,64,256]{2,1,0:T(8,128)S(1)}, u32[]{:S(2)}, u32[]{:S(2)}) %collective-permute-start.12) | collective-permute-done | bytes 262176 | tf_op jit(solution)/shard_map/ppermute | solution.py:26
  45.0 3.0 %collective-permute-start.14 = (f32[4,64,256]{2,1,0:T(8,128)S(1)}, f32[4,64,256]{2,1,0:T(8,128)}, u32[]{:S(2)}, u32[]{:S(2)}) collective-permute-start(f32[4,64,256]{2,1,0:T(8,128)S(1)} %collective-permute-done.12.rows_yl_ref), channel_id=1, source_target_pairs={{0,8},{1,9},{2,10},{3,11},{4,12},{5,13},{6,14},{7,15},{8,0},{9,1},... | collective-permute-start | bytes 786440 | tf_op jit(solution)/shard_map/ppermute | solution.py:26
  48.0 1.4 %collective-permute-start.20 = (f32[4,64,256]{2,1,0:T(8,128)S(1)}, f32[4,64,256]{2,1,0:T(8,128)}, u32[]{:S(2)}, u32[]{:S(2)}) collective-permute-start(f32[4,64,256]{2,1,0:T(8,128)S(1)} %collective-permute-done.16.refs_3_), channel_id=1, source_target_pairs={{0,8},{1,9},{2,10},{3,11},{4,12},{5,13},{6,14},{7,15},{8,0},{9,1},... | collective-permute-start | bytes 786440 | tf_op jit(solution)/shard_map/ppermute | solution.py:26
  49.5 1.2 %collective-permute-done.20.refs_7_ = f32[4,64,256]{2,1,0:T(8,128)} collective-permute-done((f32[4,64,256]{2,1,0:T(8,128)S(1)}, f32[4,64,256]{2,1,0:T(8,128)}, u32[]{:S(2)}, u32[]{:S(2)}) %collective-permute-start.20) | collective-permute-done | bytes 262176 | tf_op jit(solution)/shard_map/ppermute | solution.py:26
  50.7 2.3 %shard_map.38 = (f32[256,1024]{1,0:T(8,128)S(1)}, f32[8,8,256]{2,1,0:T(8,128)S(1)}) custom-call(s32[4]{0:T(128)S(1)} %pad_add_fusion.place_ref, f32[4,64,256]{2,1,0:T(8,128)S(1)} %pad_maximum_fusion.1.rows_ref, f32[4,64,256]{2,1,0:T(8,128)S(1)} %collective-permute-done.12.rows_yl_ref, f32[4,64,256]{2,1,0:T(8,128)S(1)} %collective-permute-done.13.rows_beside_ref, ...), custom_call_target="tpu_custom_call" | custom-call | flops 805306368 | bytes 2097152 | tf_op jit(solution)/shard_map/pallas_call | solution.py:142
  53.0 8.6 %all_to_all.5.sums_ref = f32[8,8,256]{2,1,0:T(8,128)S(1)} all-to-all(f32[8,8,256]{2,1,0:T(8,128)S(1)} %get-tuple-element.20), channel_id=1, replica_groups=mesh['yh'=2,'z'=8,'core'=2,'yl'=2,'x'=4] {'yl','x'}, dimensions={0} | all-to-all | bytes 131072 | tf_op jit(solution)/shard_map/all_to_all | solution.py:198
  61.6 1.1 %shard_map.39 = f32[256,1024]{1,0:T(8,128)} custom-call(f32[256,1024]{1,0:T(8,128)S(1)} %get-tuple-element.19.scaled_ref, f32[8,8,256]{2,1,0:T(8,128)S(1)} %all_to_all.5.sums_ref), custom_call_target="tpu_custom_call" | custom-call | bytes 2097152 | tf_op jit(solution)/shard_map/pallas_call | solution.py:142
  (25 shorter events, 0.4 us)
Async XLA Ops:
  0.0 50.7 %copy-start = (f32[256,1024]{1,0:T(8,128)S(1)}, f32[256,1024]{1,0:T(8,128)}, u32[]{:S(2)}) copy-start(f32[256,1024]{1,0:T(8,128)} %accum_ref.1) | copy-start | bytes 3145732
  0.0 4.4 %collective-permute-start.4 = (f32[64,256]{1,0:T(8,128)}, f32[64,256]{1,0:T(8,128)S(1)}, u32[]{:S(2)}, u32[]{:S(2)}) collective-permute-start(f32[64,256]{1,0:T(8,128)} %bitcast.15), channel_id=1, source_target_pairs={{0,8},{1,9},{2,10},{3,11},{4,12},{5,13},{6,14},{7,15},{8,0},{9,1},... | collective-permute-start | bytes 196616 | tf_op jit(solution)/shard_map/ppermute | solution.py:26
  5.2 8.4 %collective-permute-start.5 = (f32[2,64,256]{2,1,0:T(8,128)S(1)}, f32[2,64,256]{2,1,0:T(8,128)S(1)}, u32[]{:S(2)}, u32[]{:S(2)}) collective-permute-start(f32[2,64,256]{2,1,0:T(8,128)S(1)} %pad_maximum_fusion.2), channel_id=1, source_target_pairs={{0,32},{1,33},{2,34},{3,35},{4,160},{5,161},{6,162},{7,163},{8,104... | collective-permute-start | bytes 393224 | tf_op jit(solution)/shard_map/ppermute | solution.py:26
  9.6 8.0 %collective-permute-start.2 = (f32[64,256]{1,0:T(8,128)}, f32[64,256]{1,0:T(8,128)S(1)}, u32[]{:S(2)}, u32[]{:S(2)}) collective-permute-start(f32[64,256]{1,0:T(8,128)} %bitcast.17), channel_id=1, source_target_pairs={{0,64},{1,65},{2,66},{3,67},{4,192},{5,193},{6,194},{7,195},{8,72}... | collective-permute-start | bytes 196616 | tf_op jit(solution)/shard_map/ppermute | solution.py:26
  10.6 7.4 %collective-permute-start = (f32[64,256]{1,0:T(8,128)}, f32[64,256]{1,0:T(8,128)S(1)}, u32[]{:S(2)}, u32[]{:S(2)}) collective-permute-start(f32[64,256]{1,0:T(8,128)} %bitcast.18), channel_id=1, source_target_pairs={{0,0},{1,1},{2,2},{3,3},{4,128},{5,129},{6,130},{7,131},{8,8},{9,9... | collective-permute-start | bytes 196616 | tf_op jit(solution)/shard_map/ppermute | solution.py:26
  13.6 5.6 %collective-permute-start.6 = (f32[2,64,256]{2,1,0:T(8,128)S(1)}, f32[2,64,256]{2,1,0:T(8,128)S(1)}, u32[]{:S(2)}, u32[]{:S(2)}) collective-permute-start(f32[2,64,256]{2,1,0:T(8,128)S(1)} %collective-permute-done.5.near_ref), channel_id=1, source_target_pairs={{0,8},{1,9},{2,10},{3,11},{4,12},{5,13},{6,14},{7,15},{8,0},{9,1},... | collective-permute-start | bytes 393224 | tf_op jit(solution)/shard_map/ppermute | solution.py:26
  17.6 1.3 %collective-permute-start.3 = (f32[64,256]{1,0:T(8,128)S(1)}, f32[64,256]{1,0:T(8,128)S(1)}, u32[]{:S(2)}, u32[]{:S(2)}) collective-permute-start(f32[64,256]{1,0:T(8,128)S(1)} %collective-permute-done.2.far_ref), channel_id=1, source_target_pairs={{0,8},{1,9},{2,10},{3,11},{4,12},{5,13},{6,14},{7,15},{8,0},{9,1},... | collective-permute-start | bytes 196616 | tf_op jit(solution)/shard_map/ppermute | solution.py:26
  17.9 1.3 %collective-permute-start.1 = (f32[64,256]{1,0:T(8,128)S(1)}, f32[64,256]{1,0:T(8,128)S(1)}, u32[]{:S(2)}, u32[]{:S(2)}) collective-permute-start(f32[64,256]{1,0:T(8,128)S(1)} %collective-permute-done.here_ref), channel_id=1, source_target_pairs={{0,8},{1,9},{2,10},{3,11},{4,12},{5,13},{6,14},{7,15},{8,0},{9,1},... | collective-permute-start | bytes 196616 | tf_op jit(solution)/shard_map/ppermute | solution.py:26
  19.8 8.2 %collective-permute-start.7 = (f32[2,64,256]{2,1,0:T(8,128)S(1)}, f32[2,64,256]{2,1,0:T(8,128)S(1)}, u32[]{:S(2)}, u32[]{:S(2)}) collective-permute-start(f32[2,64,256]{2,1,0:T(8,128)S(1)} %get-tuple-element.14), channel_id=1, source_target_pairs={{0,1},{1,2},{2,3},{3,0},{4,5},{5,6},{6,7},{7,4},{8,11},{9,8},{10,9... | collective-permute-start | bytes 393224 | tf_op jit(solution)/shard_map/ppermute | solution.py:26
  22.3 5.6 %collective-permute-start.8 = (f32[64,256]{1,0:T(8,128)S(1)}, f32[64,256]{1,0:T(8,128)S(1)}, u32[]{:S(2)}, u32[]{:S(2)}) collective-permute-start(f32[64,256]{1,0:T(8,128)S(1)} %get-tuple-element.15), channel_id=1, source_target_pairs={{0,2},{1,3},{2,0},{3,1},{4,6},{5,7},{6,4},{7,5},{8,10},{9,11},{10,... | collective-permute-start | bytes 196616 | tf_op jit(solution)/shard_map/ppermute | solution.py:26
  28.0 5.6 %copy-start.2 = (f32[256,64]{0,1:T(8,128)S(1)}, f32[256,64]{0,1:T(8,128)}, u32[]{:S(2)}) copy-start(f32[256,64]{0,1:T(8,128)} %param.3) | copy-start | bytes 196612
  28.0 11.1 %collective-permute-start.9 = (f32[4,64,256]{2,1,0:T(8,128)S(1)}, f32[4,64,256]{2,1,0:T(8,128)S(1)}, u32[]{:S(2)}, u32[]{:S(2)}) collective-permute-start(f32[4,64,256]{2,1,0:T(8,128)S(1)} %pad_maximum_fusion.refs_0_), channel_id=1, source_target_pairs={{0,128},{1,129},{2,130},{3,131},{4,132},{5,133},{6,134},{7,135},{8... | collective-permute-start | bytes 786440 | tf_op jit(solution)/shard_map/ppermute | solution.py:26
  32.7 6.4 %collective-permute-start.10 = (f32[2,64,256]{2,1,0:T(8,128)S(1)}, f32[2,64,256]{2,1,0:T(8,128)S(1)}, u32[]{:S(2)}, u32[]{:S(2)}) collective-permute-start(f32[2,64,256]{2,1,0:T(8,128)S(1)} %pad_maximum_fusion.2), channel_id=1, source_target_pairs={{0,1},{1,2},{2,3},{3,0},{4,5},{5,6},{6,7},{7,4},{8,11},{9,8},{10,9... | collective-permute-start | bytes 393224 | tf_op jit(solution)/shard_map/ppermute | solution.py:26
  33.6 5.6 %collective-permute-start.11 = (f32[64,256]{1,0:T(8,128)S(1)}, f32[64,256]{1,0:T(8,128)S(1)}, u32[]{:S(2)}, u32[]{:S(2)}) collective-permute-start(f32[64,256]{1,0:T(8,128)S(1)} %bitcast.19), channel_id=1, source_target_pairs={{0,2},{1,3},{2,0},{3,1},{4,6},{5,7},{6,4},{7,5},{8,10},{9,11},{10,... | collective-permute-start | bytes 196616 | tf_op jit(solution)/shard_map/ppermute | solution.py:26
  33.6 9.4 %collective-permute-start.17 = (f32[4,64,256]{2,1,0:T(8,128)S(1)}, f32[4,64,256]{2,1,0:T(8,128)S(1)}, u32[]{:S(2)}, u32[]{:S(2)}) collective-permute-start(f32[4,64,256]{2,1,0:T(8,128)S(1)} %pad_maximum_fusion.refs_0_), channel_id=1, source_target_pairs={{0,8},{1,9},{2,10},{3,11},{4,12},{5,13},{6,14},{7,15},{8,0},{9,1},... | collective-permute-start | bytes 786440 | tf_op jit(solution)/shard_map/ppermute | solution.py:26
  35.8 7.2 %collective-permute-start.15 = (f32[4,64,256]{2,1,0:T(8,128)S(1)}, f32[4,64,256]{2,1,0:T(8,128)S(1)}, u32[]{:S(2)}, u32[]{:S(2)}) collective-permute-start(f32[4,64,256]{2,1,0:T(8,128)S(1)} %pad_maximum_fusion.refs_0_), channel_id=1, source_target_pairs={{0,16},{1,17},{2,18},{3,19},{4,20},{5,21},{6,22},{7,23},{8,120},{9... | collective-permute-start | bytes 786440 | tf_op jit(solution)/shard_map/ppermute | solution.py:26
  39.2 5.8 %collective-permute-start.12 = (f32[4,64,256]{2,1,0:T(8,128)S(1)}, f32[4,64,256]{2,1,0:T(8,128)S(1)}, u32[]{:S(2)}, u32[]{:S(2)}) collective-permute-start(f32[4,64,256]{2,1,0:T(8,128)S(1)} %pad_maximum_fusion.1.rows_ref), channel_id=1, source_target_pairs={{0,4},{1,5},{2,6},{3,7},{4,0},{5,1},{6,2},{7,3},{8,12},{9,13},{10,... | collective-permute-start | bytes 786440 | tf_op jit(solution)/shard_map/ppermute | solution.py:26
  39.8 8.2 %collective-permute-start.16 = (f32[4,64,256]{2,1,0:T(8,128)S(1)}, f32[4,64,256]{2,1,0:T(8,128)S(1)}, u32[]{:S(2)}, u32[]{:S(2)}) collective-permute-start(f32[4,64,256]{2,1,0:T(8,128)S(1)} %collective-permute-done.9.refs_1_), channel_id=1, source_target_pairs={{0,16},{1,17},{2,18},{3,19},{4,20},{5,21},{6,22},{7,23},{8,120},{9... | collective-permute-start | bytes 786440 | tf_op jit(solution)/shard_map/ppermute | solution.py:26
  41.5 8.0 %collective-permute-start.13 = (f32[4,64,256]{2,1,0:T(8,128)S(1)}, f32[4,64,256]{2,1,0:T(8,128)S(1)}, u32[]{:S(2)}, u32[]{:S(2)}) collective-permute-start(f32[4,64,256]{2,1,0:T(8,128)S(1)} %pad_maximum_fusion.1.rows_ref), channel_id=1, source_target_pairs={{0,8},{1,9},{2,10},{3,11},{4,12},{5,13},{6,14},{7,15},{8,0},{9,1},... | collective-permute-start | bytes 786440 | tf_op jit(solution)/shard_map/ppermute | solution.py:26
  43.0 6.5 %collective-permute-start.18 = (f32[4,64,256]{2,1,0:T(8,128)S(1)}, f32[4,64,256]{2,1,0:T(8,128)S(1)}, u32[]{:S(2)}, u32[]{:S(2)}) collective-permute-start(f32[4,64,256]{2,1,0:T(8,128)S(1)} %collective-permute-done.9.refs_1_), channel_id=1, source_target_pairs={{0,8},{1,9},{2,10},{3,11},{4,12},{5,13},{6,14},{7,15},{8,0},{9,1},... | collective-permute-start | bytes 786440 | tf_op jit(solution)/shard_map/ppermute | solution.py:26
  43.0 6.5 %collective-permute-start.19 = (f32[4,64,256]{2,1,0:T(8,128)S(1)}, f32[4,64,256]{2,1,0:T(8,128)}, u32[]{:S(2)}, u32[]{:S(2)}) collective-permute-start(f32[4,64,256]{2,1,0:T(8,128)S(1)} %collective-permute-done.15.refs_2_), channel_id=1, source_target_pairs={{0,8},{1,9},{2,10},{3,11},{4,12},{5,13},{6,14},{7,15},{8,0},{9,1},... | collective-permute-start | bytes 786440 | tf_op jit(solution)/shard_map/ppermute | solution.py:26
  45.0 4.5 %collective-permute-start.14 = (f32[4,64,256]{2,1,0:T(8,128)S(1)}, f32[4,64,256]{2,1,0:T(8,128)}, u32[]{:S(2)}, u32[]{:S(2)}) collective-permute-start(f32[4,64,256]{2,1,0:T(8,128)S(1)} %collective-permute-done.12.rows_yl_ref), channel_id=1, source_target_pairs={{0,8},{1,9},{2,10},{3,11},{4,12},{5,13},{6,14},{7,15},{8,0},{9,1},... | collective-permute-start | bytes 786440 | tf_op jit(solution)/shard_map/ppermute | solution.py:26
  48.0 2.7 %collective-permute-start.20 = (f32[4,64,256]{2,1,0:T(8,128)S(1)}, f32[4,64,256]{2,1,0:T(8,128)}, u32[]{:S(2)}, u32[]{:S(2)}) collective-permute-start(f32[4,64,256]{2,1,0:T(8,128)S(1)} %collective-permute-done.16.refs_3_), channel_id=1, source_target_pairs={{0,8},{1,9},{2,10},{3,11},{4,12},{5,13},{6,14},{7,15},{8,0},{9,1},... | collective-permute-start | bytes 786440 | tf_op jit(solution)/shard_map/ppermute | solution.py:26
  49.4 1.3 %copy-start.1 = (f32[1024]{0:T(1024)S(1)}, f32[1024]{0:T(1024)}, u32[]{:S(2)}) copy-start(f32[1024]{0:T(1024)} %param.5) | copy-start | bytes 12292

commit v4 on v3

v4 whole, which is shorter than its diff:
```python
import itertools

import jax
import jax.numpy as jnp
from jax import lax
from jax.experimental import pallas as pl
from jax.experimental.pallas import tpu as pltpu
from jax.sharding import Mesh, PartitionSpec as P

YH, Z, CORE, YL, X = SIZES = 2, 8, 2, 2, 4
ROW = ("yh", "z", "core")
COL = ("yl", "x")
ALL = (*ROW, *COL)
VMEM = pl.BlockSpec(memory_space=pltpu.VMEM)
SMEM = pl.BlockSpec(memory_space=pltpu.SMEM)


def send(value, target):
    def index(place):
        found = 0
        for at, size in zip(place, SIZES, strict=True):
            found = found * size + at
        return found

    pairs = [(index(place), index(target(*place))) for place in itertools.product(*map(range, SIZES))]
    return lax.ppermute(value, ALL, pairs)


def across(yh, z, core, yl, x):
    return yh, z, 1 - core, yl, x


def along_z(hops):
    def target(yh, z, core, yl, x):
        return yl, (z + hops) % Z, core, yh, x

    return target


def pass_on(yh, z, core, yl, x):
    return yh, (z + (1 if core == 0 else -1)) % Z, core, yl, x


def along_x(hops):
    def target(yh, z, core, yl, x):
        return yh, z, core, yl, (x + hops) % X

    return target


def along_y(yh, z, core, yl, x):
    return 1 - yh, z, core, yl, x


def diagonal(yh, z, core, yl, x):
    return 1 - yh, (z + (1 if core == 0 else -1)) % Z, core, yl, x


def along_yl(yh, z, core, yl, x):
    return yh, z, core, 1 - yl, x


def sort_planes(place_ref, *refs):
    held, outs, sorted_ref = refs[:X], refs[X : 2 * X], refs[2 * X]
    z, x = (place_ref[i] for i in range(2))
    for step, piece in enumerate(held):
        sorted_ref[lax.rem(z // 2 - step - x + 2 * X, X)] = piece[...]
    for step, out in enumerate(outs):
        out[...] = sorted_ref[step]


def split(value):
    high = value.astype(jnp.bfloat16)
    low = (value - high.astype(jnp.float32)).astype(jnp.bfloat16)
    return high, low


def times(a, b):
    return lax.dot_general(a, b, (((0,), (0,)), ((), ())), preferred_element_type=jnp.float32)


def product(place_ref, rows0_ref, rows1_ref, rows2_ref, rows3_ref, accum_ref, scale_ref, *refs):
    packs, (scaled_ref, sums_ref) = (refs[:4], refs[4:8]), refs[8:]
    yh, z, core, yl = (place_ref[i] for i in range(4))
    at = lax.rem(yh + yl, 2)
    held = (rows0_ref, rows1_ref, rows2_ref, rows3_ref)
    high, low = split(jnp.concatenate([ref[at] for ref in held] + [ref[1 - at] for ref in held], axis=0))
    depth = high.shape[0]
    rows, width = rows0_ref.shape[2], refs[0].shape[2]
    squares = jnp.zeros((rows, 128), jnp.float32)
    for odd in range(2):
        for beside in range(CORE):
            pair = [packs[beside][2 * odd + i][...] for i in range(2)]
            block = jnp.concatenate(pair, axis=0).reshape(depth, width)
            block_high, block_low = split(block)
            part = times(high, block_high) + (times(high, block_low) + times(low, block_high))
            tile = lax.rem(z + odd, 2) * CORE + lax.rem(core + beside, CORE)
            cols = pl.ds(pl.multiple_of(tile * width, width), width)
            scaled = (accum_ref[:, cols] + part) * scale_ref[:, cols]
            scaled_ref[:, cols] = scaled
            for lane in range(0, width, 128):
                chunk = scaled[:, lane : lane + 128]
                squares += chunk * chunk
    sums = jnp.sum(squares.T, axis=0, keepdims=True)
    sums_ref[...] = jnp.broadcast_to(sums[None], sums_ref.shape)


def divide(scaled_ref, sums_ref, out_ref):
    rows, cols = scaled_ref.shape
    total = jnp.sum(sums_ref[...], axis=0)[:1]
    count = cols * sums_ref.shape[0]
    factor = lax.rsqrt(total / count + 1e-06)
    factor = jnp.broadcast_to(factor, (128, rows)).T
    for lane in range(0, cols, 128):
        out_ref[:, lane : lane + 128] = scaled_ref[:, lane : lane + 128] * factor


def call(kernel, out_shape, inputs, scalars=1, scratch=(), flops=0):
    return pl.pallas_call(
        kernel,
        out_shape=out_shape,
        in_specs=[SMEM] * scalars + [VMEM] * (len(inputs) - scalars),
        out_specs=jax.tree.map(lambda _: VMEM, out_shape),
        scratch_shapes=list(scratch),
        compiler_params=pltpu.CompilerParams(vmem_limit_bytes=16 * 1024 * 1024),
        cost_estimate=pl.CostEstimate(flops=flops, bytes_accessed=2 * 1024 * 1024, transcendentals=0),
    )(*inputs)


def f32(*shape):
    return jax.ShapeDtypeStruct(shape, jnp.float32)


def place(*names):
    return jnp.stack([lax.axis_index(name) for name in names])


def per_device(left_panel, accum, col_scale):
    block = left_panel.T
    depth, rows = block.shape
    cols = accum.shape[1]
    groups = YL * X

    held = [send(block, along_z(2 * step)) for step in range(X)]
    beside_yl = send(block, along_yl)
    planes = call(
        sort_planes,
        (f32(depth, rows),) * X,
        [place("z", "x"), *held],
        scratch=[pltpu.VMEM((X, depth, rows), jnp.float32)],
    )
    got = [send(planes[step], along_x(step)) for step in range(1, X)]
    kept = jnp.stack([planes[0], *got])
    _, beside_yl = lax.optimization_barrier((planes[1], beside_yl))
    pair = jnp.stack([block, beside_yl])
    from_x = [send(pair, along_x(step)) for step in range(1, X)]
    other_y = send(kept, along_y)
    passed = send(kept, pass_on)
    both_passed = send(kept, diagonal)
    other_y, *from_x = lax.optimization_barrier((other_y, *from_x))
    full_rows = [pair, *from_x]
    mine = [kept, other_y, passed, both_passed]
    others = [send(pack, across) for pack in mine]

    scaled, sums = call(
        product,
        (f32(rows, cols), f32(groups, 8, rows)),
        [place("yh", "z", "core", "yl"), *full_rows, accum, col_scale[None], *mine, *others],
        flops=6 * rows * cols * depth * groups,
    )
    sums = lax.all_to_all(sums, COL, 0, 0)
    return call(divide, f32(rows, cols), [scaled, sums], scalars=0)


def solution(mesh):
    fine = Mesh(mesh.devices.reshape(SIZES), ALL)
    placed = (P(ROW, COL), P(ROW, COL), P(COL))
    return jax.shard_map(
        per_device, mesh=fine, in_specs=placed, out_specs=P(ROW, COL), check_vma=False
    )
```

time: 63 us -> 58.6 us (0.930)
  waiting for transfers between devices: 16.6 us -> 6.02 us
  starting transfers between devices: 32.4 us -> 37.3 us
  local copies, waits for them, and re-layouts: 0.01 us -> 1.57 us
    ppermute x21 -> x18, waiting for transfers between devices: 16.6 us -> 6.02 us  [send(): return lax.ppermute(value, ALL, pairs)]
    ppermute x21 -> x18, starting transfers between devices: 32.4 us -> 37.3 us  [send(): return lax.ppermute(value, ALL, pairs)]
    unnamed x6 -> x8, local copies, waits for them, and re-layouts: 0.01 us -> 1.57 us
  transfers between devices with their start and end apart: 21 -> 18, of which waited for: 9 -> 5; matrix products, arithmetic and copies ran while one was open for 0% -> 2% of each run, Pallas kernels for 0% -> 1%
where the time goes in v4:
time: 58.6 us; the launch traced here: 58.4 us
  starting transfers between devices  37.3 us (64%)
  blocking collectives  9 us (15%)
  waiting for transfers between devices  6.02 us (10%)
  Pallas kernels  3.4 us (6%)
  local copies, waits for them, and re-layouts  1.57 us (3%)
  other arithmetic  1.02 us (2%)
    ppermute x18, starting transfers between devices, send(): return lax.ppermute(value, ALL, pairs)  37.3 us
    all_to_all x1, blocking collectives, per_device(): sums = lax.all_to_all(sums, COL, 0, 0)  9 us
    ppermute x18, waiting for transfers between devices, send(): return lax.ppermute(value, ALL, pairs)  6.02 us
    pallas_call x3, Pallas kernels, call(): pl.pallas_call(kernel, out_shape=out_shape, in_specs=[SMEM] * scalars + [...  3.4 us
    unnamed x8, local copies, waits for them, and re-layouts  1.57 us
  transfers between devices with their start and end apart: 18, of which 5 were waited for; matrix products, arithmetic and copies ran while one was open for 2% of the time, Pallas kernels for 1%

profile of v4, /device:TPU:1, one launch (start us, length us, event | category | flops | bytes accessed | tf_op | source)
XLA Modules:
  0.0 58.4 jit_solution(8333834348954187111)
XLA Ops:
  0.0 6.8 %collective-permute-start.3 = (f32[64,256]{1,0:T(8,128)}, f32[64,256]{1,0:T(8,128)S(1)}, u32[]{:S(2)}, u32[]{:S(2)}) collective-permute-start(f32[64,256]{1,0:T(8,128)} %bitcast.16), channel_id=1, source_target_pairs={{0,96},{1,97},{2,98},{3,99},{4,224},{5,225},{6,226},{7,227},{8,104... | collective-permute-start | bytes 196616 | tf_op jit(solution)/shard_map/ppermute | solution.py:26
  6.9 1.0 %collective-permute-start.2 = (f32[64,256]{1,0:T(8,128)}, f32[64,256]{1,0:T(8,128)S(1)}, u32[]{:S(2)}, u32[]{:S(2)}) collective-permute-start(f32[64,256]{1,0:T(8,128)} %bitcast.17), channel_id=1, source_target_pairs={{0,64},{1,65},{2,66},{3,67},{4,192},{5,193},{6,194},{7,195},{8,72}... | collective-permute-start | bytes 196616 | tf_op jit(solution)/shard_map/ppermute | solution.py:26
  7.8 2.3 %collective-permute-start.1 = (f32[64,256]{1,0:T(8,128)}, f32[64,256]{1,0:T(8,128)S(1)}, u32[]{:S(2)}, u32[]{:S(2)}) collective-permute-start(f32[64,256]{1,0:T(8,128)} %bitcast.18), channel_id=1, source_target_pairs={{0,32},{1,33},{2,34},{3,35},{4,160},{5,161},{6,162},{7,163},{8,40}... | collective-permute-start | bytes 196616 | tf_op jit(solution)/shard_map/ppermute | solution.py:26
  10.1 1.5 %collective-permute-start = (f32[64,256]{1,0:T(8,128)}, f32[64,256]{1,0:T(8,128)S(1)}, u32[]{:S(2)}, u32[]{:S(2)}) collective-permute-start(f32[64,256]{1,0:T(8,128)} %bitcast.19), channel_id=1, source_target_pairs={{0,0},{1,1},{2,2},{3,3},{4,128},{5,129},{6,130},{7,131},{8,8},{9,9... | collective-permute-start | bytes 196616 | tf_op jit(solution)/shard_map/ppermute | solution.py:26
  11.6 3.9 %collective-permute-start.4 = (f32[64,256]{1,0:T(8,128)}, f32[64,256]{1,0:T(8,128)S(1)}, u32[]{:S(2)}, u32[]{:S(2)}) collective-permute-start(f32[64,256]{1,0:T(8,128)} %bitcast.20), channel_id=1, source_target_pairs={{0,4},{1,5},{2,6},{3,7},{4,0},{5,1},{6,2},{7,3},{8,12},{9,13},{10,... | collective-permute-start | bytes 196616 | tf_op jit(solution)/shard_map/ppermute | solution.py:26
  15.5 0.1 pad_add_fusion.1.place_ref
  15.6 0.6 %shard_map.37 = (f32[64,256]{1,0:T(8,128)S(1)}, f32[64,256]{1,0:T(8,128)S(1)}, f32[64,256]{1,0:T(8,128)S(1)}, f32[64,256]{1,0:T(8,128)S(1)}) custom-call(s32[2]{0:T(128)S(1)} %pad_add_fusion.1.place_ref, f32[64,256]{1,0:T(8,128)S(1)} %collective-permute-done.refs_0_, f32[64,256]{1,0:T(8,128)S(1)} %collective-permute-done.1.refs_1_, ...), custom_call_target="tpu_custom_call" | custom-call | bytes 2097152 | tf_op jit(solution)/shard_map/pallas_call | solution.py:119
  16.2 2.8 %collective-permute-start.6 = (f32[64,256]{1,0:T(8,128)S(1)}, f32[64,256]{1,0:T(8,128)S(1)}, u32[]{:S(2)}, u32[]{:S(2)}) collective-permute-start(f32[64,256]{1,0:T(8,128)S(1)} %get-tuple-element.19), channel_id=1, source_target_pairs={{0,2},{1,3},{2,0},{3,1},{4,6},{5,7},{6,4},{7,5},{8,10},{9,11},{10,... | collective-permute-start | bytes 196616 | tf_op jit(solution)/shard_map/ppermute | solution.py:26
  19.0 0.9 %collective-permute-start.7 = (f32[64,256]{1,0:T(8,128)S(1)}, f32[64,256]{1,0:T(8,128)S(1)}, u32[]{:S(2)}, u32[]{:S(2)}) collective-permute-start(f32[64,256]{1,0:T(8,128)S(1)} %get-tuple-element.20), channel_id=1, source_target_pairs={{0,3},{1,0},{2,1},{3,2},{4,7},{5,4},{6,5},{7,6},{8,11},{9,8},{10,9... | collective-permute-start | bytes 196616 | tf_op jit(solution)/shard_map/ppermute | solution.py:26
  19.9 0.6 %collective-permute-start.5 = (f32[64,256]{1,0:T(8,128)S(1)}, f32[64,256]{1,0:T(8,128)S(1)}, u32[]{:S(2)}, u32[]{:S(2)}) collective-permute-start(f32[64,256]{1,0:T(8,128)S(1)} %get-tuple-element.16), channel_id=1, source_target_pairs={{0,1},{1,2},{2,3},{3,0},{4,5},{5,6},{6,7},{7,4},{8,9},{9,10},{10,1... | collective-permute-start | bytes 196616 | tf_op jit(solution)/shard_map/ppermute | solution.py:26
  20.5 0.8 %pad_maximum_fusion.1.rows0_ref = f32[2,64,256]{2,1,0:T(8,128)S(1)} fusion(f32[1,64,256]{2,1,0:T(8,128)S(1)} %bitcast.22, f32[1,64,256]{2,1,0:T(8,128)} %bitcast.21), kind=kLoop, calls=%fused_computation.1 | loop fusion | flops 32768 | bytes 262144 | tf_op jit(solution)/shard_map/stack | solution.py:155
  21.3 2.1 %collective-permute-start.11 = (f32[2,64,256]{2,1,0:T(8,128)S(1)}, f32[2,64,256]{2,1,0:T(8,128)S(1)}, u32[]{:S(2)}, u32[]{:S(2)}) collective-permute-start(f32[2,64,256]{2,1,0:T(8,128)S(1)} %pad_maximum_fusion.1.rows0_ref), channel_id=1, source_target_pairs={{0,3},{1,0},{2,1},{3,2},{4,7},{5,4},{6,5},{7,6},{8,11},{9,8},{10,9... | collective-permute-start | bytes 393224 | tf_op jit(solution)/shard_map/ppermute | solution.py:26
  23.5 0.7 %collective-permute-done.5 = f32[64,256]{1,0:T(8,128)S(1)} collective-permute-done((f32[64,256]{1,0:T(8,128)S(1)}, f32[64,256]{1,0:T(8,128)S(1)}, u32[]{:S(2)}, u32[]{:S(2)}) %collective-permute-start.5) | collective-permute-done | bytes 65568 | tf_op jit(solution)/shard_map/ppermute | solution.py:26
  24.2 5.5 %collective-permute-start.8 = (f32[4,64,256]{2,1,0:T(8,128)S(1)}, f32[4,64,256]{2,1,0:T(8,128)S(1)}, u32[]{:S(2)}, u32[]{:S(2)}) collective-permute-start(f32[4,64,256]{2,1,0:T(8,128)S(1)} %pad_maximum_fusion.refs_0_), channel_id=1, source_target_pairs={{0,128},{1,129},{2,130},{3,131},{4,132},{5,133},{6,134},{7,135},{8... | collective-permute-start | bytes 786440 | tf_op jit(solution)/shard_map/ppermute | solution.py:26
  29.7 1.2 %collective-permute-start.13 = (f32[4,64,256]{2,1,0:T(8,128)S(1)}, f32[4,64,256]{2,1,0:T(8,128)S(1)}, u32[]{:S(2)}, u32[]{:S(2)}) collective-permute-start(f32[4,64,256]{2,1,0:T(8,128)S(1)} %pad_maximum_fusion.refs_0_), channel_id=1, source_target_pairs={{0,144},{1,145},{2,146},{3,147},{4,148},{5,149},{6,150},{7,151},{8... | collective-permute-start | bytes 786440 | tf_op jit(solution)/shard_map/ppermute | solution.py:26
  30.9 1.4 %collective-permute-start.12 = (f32[4,64,256]{2,1,0:T(8,128)S(1)}, f32[4,64,256]{2,1,0:T(8,128)S(1)}, u32[]{:S(2)}, u32[]{:S(2)}) collective-permute-start(f32[4,64,256]{2,1,0:T(8,128)S(1)} %pad_maximum_fusion.refs_0_), channel_id=1, source_target_pairs={{0,16},{1,17},{2,18},{3,19},{4,20},{5,21},{6,22},{7,23},{8,120},{9... | collective-permute-start | bytes 786440 | tf_op jit(solution)/shard_map/ppermute | solution.py:26
  32.3 1.0 %collective-permute-start.10 = (f32[2,64,256]{2,1,0:T(8,128)S(1)}, f32[2,64,256]{2,1,0:T(8,128)S(1)}, u32[]{:S(2)}, u32[]{:S(2)}) collective-permute-start(f32[2,64,256]{2,1,0:T(8,128)S(1)} %pad_maximum_fusion.1.rows0_ref), channel_id=1, source_target_pairs={{0,2},{1,3},{2,0},{3,1},{4,6},{5,7},{6,4},{7,5},{8,10},{9,11},{10,... | collective-permute-start | bytes 393224 | tf_op jit(solution)/shard_map/ppermute | solution.py:26
  33.2 0.7 %collective-permute-start.9 = (f32[2,64,256]{2,1,0:T(8,128)S(1)}, f32[2,64,256]{2,1,0:T(8,128)S(1)}, u32[]{:S(2)}, u32[]{:S(2)}) collective-permute-start(f32[2,64,256]{2,1,0:T(8,128)S(1)} %pad_maximum_fusion.1.rows0_ref), channel_id=1, source_target_pairs={{0,1},{1,2},{2,3},{3,0},{4,5},{5,6},{6,7},{7,4},{8,9},{9,10},{10,1... | collective-permute-start | bytes 393224 | tf_op jit(solution)/shard_map/ppermute | solution.py:26
  33.9 4.0 %collective-permute-done.10.rows2_ref = f32[2,64,256]{2,1,0:T(8,128)S(1)} collective-permute-done((f32[2,64,256]{2,1,0:T(8,128)S(1)}, f32[2,64,256]{2,1,0:T(8,128)S(1)}, u32[]{:S(2)}, u32[]{:S(2)}) %collective-permute-start.10) | collective-permute-done | bytes 131104 | tf_op jit(solution)/shard_map/ppermute | solution.py:26
  37.9 3.9 %collective-permute-start.14 = (f32[4,64,256]{2,1,0:T(8,128)S(1)}, f32[4,64,256]{2,1,0:T(8,128)S(1)}, u32[]{:S(2)}, u32[]{:S(2)}) collective-permute-start(f32[4,64,256]{2,1,0:T(8,128)S(1)} %pad_maximum_fusion.refs_0_), channel_id=1, source_target_pairs={{0,8},{1,9},{2,10},{3,11},{4,12},{5,13},{6,14},{7,15},{8,0},{9,1},... | collective-permute-start | bytes 786440 | tf_op jit(solution)/shard_map/ppermute | solution.py:26
  41.8 0.7 %copy-done.1 = f32[2,64,256]{2,1,0:T(8,128)} copy-done((f32[2,64,256]{2,1,0:T(8,128)}, f32[2,64,256]{2,1,0:T(8,128)S(1)}, u32[]{:S(2)}) %copy-start.1) | copy-done | bytes 131096
  42.4 1.3 %collective-permute-start.17 = (f32[4,64,256]{2,1,0:T(8,128)S(1)}, f32[4,64,256]{2,1,0:T(8,128)S(1)}, u32[]{:S(2)}, u32[]{:S(2)}) collective-permute-start(f32[4,64,256]{2,1,0:T(8,128)S(1)} %collective-permute-done.13.refs_3_), channel_id=1, source_target_pairs={{0,8},{1,9},{2,10},{3,11},{4,12},{5,13},{6,14},{7,15},{8,0},{9,1},... | collective-permute-start | bytes 786440 | tf_op jit(solution)/shard_map/ppermute | solution.py:26
  43.7 0.1 collective-permute-start.16
  43.8 0.4 collective-permute-start.15
  44.2 0.1 pad_add_fusion.place_ref
  44.3 0.6 collective-permute-done.17.refs_7_
  44.9 0.4 collective-permute-done.16.refs_6_
  45.3 0.4 collective-permute-done.15.refs_5_
  45.6 0.9 %copy-done.2 = f32[2,64,256]{2,1,0:T(8,128)S(1)} copy-done((f32[2,64,256]{2,1,0:T(8,128)S(1)}, f32[2,64,256]{2,1,0:T(8,128)}, u32[]{:S(2)}) %copy-start.2) | copy-done | bytes 131096
  46.5 1.7 %shard_map.38 = (f32[256,1024]{1,0:T(8,128)S(1)}, f32[8,8,256]{2,1,0:T(8,128)S(1)}) custom-call(s32[4]{0:T(128)S(1)} %pad_add_fusion.place_ref, f32[2,64,256]{2,1,0:T(8,128)S(1)} %pad_maximum_fusion.1.rows0_ref, f32[2,64,256]{2,1,0:T(8,128)S(1)} %copy-done.2, f32[2,64,256]{2,1,0:T(8,128)S(1)} %collective-permute-done.10.rows2_ref, ...), custom_call_target="tpu_custom_call" | custom-call | flops 805306368 | bytes 2097152 | tf_op jit(solution)/shard_map/pallas_call | solution.py:119
  48.2 9.0 %all_to_all.5.sums_ref = f32[8,8,256]{2,1,0:T(8,128)S(1)} all-to-all(f32[8,8,256]{2,1,0:T(8,128)S(1)} %get-tuple-element.26), channel_id=1, replica_groups=mesh['yh'=2,'z'=8,'core'=2,'yl'=2,'x'=4] {'yl','x'}, dimensions={0} | all-to-all | bytes 131072 | tf_op jit(solution)/shard_map/all_to_all | solution.py:171
  57.2 1.1 %shard_map.39 = f32[256,1024]{1,0:T(8,128)} custom-call(f32[256,1024]{1,0:T(8,128)S(1)} %get-tuple-element.25.scaled_ref, f32[8,8,256]{2,1,0:T(8,128)S(1)} %all_to_all.5.sums_ref), custom_call_target="tpu_custom_call" | custom-call | bytes 2097152 | tf_op jit(solution)/shard_map/pallas_call | solution.py:119
  (20 shorter events, 0.1 us)
Async XLA Ops:
  0.0 45.6 %copy-start = (f32[256,1024]{1,0:T(8,128)S(1)}, f32[256,1024]{1,0:T(8,128)}, u32[]{:S(2)}) copy-start(f32[256,1024]{1,0:T(8,128)} %accum_ref.1) | copy-start | bytes 3145732
  0.0 15.6 %collective-permute-start.3 = (f32[64,256]{1,0:T(8,128)}, f32[64,256]{1,0:T(8,128)S(1)}, u32[]{:S(2)}, u32[]{:S(2)}) collective-permute-start(f32[64,256]{1,0:T(8,128)} %bitcast.16), channel_id=1, source_target_pairs={{0,96},{1,97},{2,98},{3,99},{4,224},{5,225},{6,226},{7,227},{8,104... | collective-permute-start | bytes 196616 | tf_op jit(solution)/shard_map/ppermute | solution.py:26
  6.9 8.7 %collective-permute-start.2 = (f32[64,256]{1,0:T(8,128)}, f32[64,256]{1,0:T(8,128)S(1)}, u32[]{:S(2)}, u32[]{:S(2)}) collective-permute-start(f32[64,256]{1,0:T(8,128)} %bitcast.17), channel_id=1, source_target_pairs={{0,64},{1,65},{2,66},{3,67},{4,192},{5,193},{6,194},{7,195},{8,72}... | collective-permute-start | bytes 196616 | tf_op jit(solution)/shard_map/ppermute | solution.py:26
  7.8 7.7 %collective-permute-start.1 = (f32[64,256]{1,0:T(8,128)}, f32[64,256]{1,0:T(8,128)S(1)}, u32[]{:S(2)}, u32[]{:S(2)}) collective-permute-start(f32[64,256]{1,0:T(8,128)} %bitcast.18), channel_id=1, source_target_pairs={{0,32},{1,33},{2,34},{3,35},{4,160},{5,161},{6,162},{7,163},{8,40}... | collective-permute-start | bytes 196616 | tf_op jit(solution)/shard_map/ppermute | solution.py:26
  10.1 5.5 %collective-permute-start = (f32[64,256]{1,0:T(8,128)}, f32[64,256]{1,0:T(8,128)S(1)}, u32[]{:S(2)}, u32[]{:S(2)}) collective-permute-start(f32[64,256]{1,0:T(8,128)} %bitcast.19), channel_id=1, source_target_pairs={{0,0},{1,1},{2,2},{3,3},{4,128},{5,129},{6,130},{7,131},{8,8},{9,9... | collective-permute-start | bytes 196616 | tf_op jit(solution)/shard_map/ppermute | solution.py:26
  11.6 8.9 %collective-permute-start.4 = (f32[64,256]{1,0:T(8,128)}, f32[64,256]{1,0:T(8,128)S(1)}, u32[]{:S(2)}, u32[]{:S(2)}) collective-permute-start(f32[64,256]{1,0:T(8,128)} %bitcast.20), channel_id=1, source_target_pairs={{0,4},{1,5},{2,6},{3,7},{4,0},{5,1},{6,2},{7,3},{8,12},{9,13},{10,... | collective-permute-start | bytes 196616 | tf_op jit(solution)/shard_map/ppermute | solution.py:26
  16.2 7.3 %collective-permute-start.6 = (f32[64,256]{1,0:T(8,128)S(1)}, f32[64,256]{1,0:T(8,128)S(1)}, u32[]{:S(2)}, u32[]{:S(2)}) collective-permute-start(f32[64,256]{1,0:T(8,128)S(1)} %get-tuple-element.19), channel_id=1, source_target_pairs={{0,2},{1,3},{2,0},{3,1},{4,6},{5,7},{6,4},{7,5},{8,10},{9,11},{10,... | collective-permute-start | bytes 196616 | tf_op jit(solution)/shard_map/ppermute | solution.py:26
  19.0 4.5 %collective-permute-start.7 = (f32[64,256]{1,0:T(8,128)S(1)}, f32[64,256]{1,0:T(8,128)S(1)}, u32[]{:S(2)}, u32[]{:S(2)}) collective-permute-start(f32[64,256]{1,0:T(8,128)S(1)} %get-tuple-element.20), channel_id=1, source_target_pairs={{0,3},{1,0},{2,1},{3,2},{4,7},{5,4},{6,5},{7,6},{8,11},{9,8},{10,9... | collective-permute-start | bytes 196616 | tf_op jit(solution)/shard_map/ppermute | solution.py:26
  19.9 4.3 %collective-permute-start.5 = (f32[64,256]{1,0:T(8,128)S(1)}, f32[64,256]{1,0:T(8,128)S(1)}, u32[]{:S(2)}, u32[]{:S(2)}) collective-permute-start(f32[64,256]{1,0:T(8,128)S(1)} %get-tuple-element.16), channel_id=1, source_target_pairs={{0,1},{1,2},{2,3},{3,0},{4,5},{5,6},{6,7},{7,4},{8,9},{9,10},{10,1... | collective-permute-start | bytes 196616 | tf_op jit(solution)/shard_map/ppermute | solution.py:26
  21.3 11.9 %collective-permute-start.11 = (f32[2,64,256]{2,1,0:T(8,128)S(1)}, f32[2,64,256]{2,1,0:T(8,128)S(1)}, u32[]{:S(2)}, u32[]{:S(2)}) collective-permute-start(f32[2,64,256]{2,1,0:T(8,128)S(1)} %pad_maximum_fusion.1.rows0_ref), channel_id=1, source_target_pairs={{0,3},{1,0},{2,1},{3,2},{4,7},{5,4},{6,5},{7,6},{8,11},{9,8},{10,9... | collective-permute-start | bytes 393224 | tf_op jit(solution)/shard_map/ppermute | solution.py:26
  24.2 18.2 %collective-permute-start.8 = (f32[4,64,256]{2,1,0:T(8,128)S(1)}, f32[4,64,256]{2,1,0:T(8,128)S(1)}, u32[]{:S(2)}, u32[]{:S(2)}) collective-permute-start(f32[4,64,256]{2,1,0:T(8,128)S(1)} %pad_maximum_fusion.refs_0_), channel_id=1, source_target_pairs={{0,128},{1,129},{2,130},{3,131},{4,132},{5,133},{6,134},{7,135},{8... | collective-permute-start | bytes 786440 | tf_op jit(solution)/shard_map/ppermute | solution.py:26
  29.7 12.7 %collective-permute-start.13 = (f32[4,64,256]{2,1,0:T(8,128)S(1)}, f32[4,64,256]{2,1,0:T(8,128)S(1)}, u32[]{:S(2)}, u32[]{:S(2)}) collective-permute-start(f32[4,64,256]{2,1,0:T(8,128)S(1)} %pad_maximum_fusion.refs_0_), channel_id=1, source_target_pairs={{0,144},{1,145},{2,146},{3,147},{4,148},{5,149},{6,150},{7,151},{8... | collective-permute-start | bytes 786440 | tf_op jit(solution)/shard_map/ppermute | solution.py:26
  30.9 12.8 %collective-permute-start.12 = (f32[4,64,256]{2,1,0:T(8,128)S(1)}, f32[4,64,256]{2,1,0:T(8,128)S(1)}, u32[]{:S(2)}, u32[]{:S(2)}) collective-permute-start(f32[4,64,256]{2,1,0:T(8,128)S(1)} %pad_maximum_fusion.refs_0_), channel_id=1, source_target_pairs={{0,16},{1,17},{2,18},{3,19},{4,20},{5,21},{6,22},{7,23},{8,120},{9... | collective-permute-start | bytes 786440 | tf_op jit(solution)/shard_map/ppermute | solution.py:26
  32.3 5.6 %collective-permute-start.10 = (f32[2,64,256]{2,1,0:T(8,128)S(1)}, f32[2,64,256]{2,1,0:T(8,128)S(1)}, u32[]{:S(2)}, u32[]{:S(2)}) collective-permute-start(f32[2,64,256]{2,1,0:T(8,128)S(1)} %pad_maximum_fusion.1.rows0_ref), channel_id=1, source_target_pairs={{0,2},{1,3},{2,0},{3,1},{4,6},{5,7},{6,4},{7,5},{8,10},{9,11},{10,... | collective-permute-start | bytes 393224 | tf_op jit(solution)/shard_map/ppermute | solution.py:26
  33.2 8.5 %collective-permute-start.9 = (f32[2,64,256]{2,1,0:T(8,128)S(1)}, f32[2,64,256]{2,1,0:T(8,128)S(1)}, u32[]{:S(2)}, u32[]{:S(2)}) collective-permute-start(f32[2,64,256]{2,1,0:T(8,128)S(1)} %pad_maximum_fusion.1.rows0_ref), channel_id=1, source_target_pairs={{0,1},{1,2},{2,3},{3,0},{4,5},{5,6},{6,7},{7,4},{8,9},{9,10},{10,1... | collective-permute-start | bytes 393224 | tf_op jit(solution)/shard_map/ppermute | solution.py:26
  37.9 6.4 %collective-permute-start.14 = (f32[4,64,256]{2,1,0:T(8,128)S(1)}, f32[4,64,256]{2,1,0:T(8,128)S(1)}, u32[]{:S(2)}, u32[]{:S(2)}) collective-permute-start(f32[4,64,256]{2,1,0:T(8,128)S(1)} %pad_maximum_fusion.refs_0_), channel_id=1, source_target_pairs={{0,8},{1,9},{2,10},{3,11},{4,12},{5,13},{6,14},{7,15},{8,0},{9,1},... | collective-permute-start | bytes 786440 | tf_op jit(solution)/shard_map/ppermute | solution.py:26
  41.8 0.7 %copy-start.1 = (f32[2,64,256]{2,1,0:T(8,128)}, f32[2,64,256]{2,1,0:T(8,128)S(1)}, u32[]{:S(2)}) copy-start(f32[2,64,256]{2,1,0:T(8,128)S(1)} %collective-permute-done.9.rows1_ref) | copy-start | bytes 393220
  42.4 2.5 %collective-permute-start.17 = (f32[4,64,256]{2,1,0:T(8,128)S(1)}, f32[4,64,256]{2,1,0:T(8,128)S(1)}, u32[]{:S(2)}, u32[]{:S(2)}) collective-permute-start(f32[4,64,256]{2,1,0:T(8,128)S(1)} %collective-permute-done.13.refs_3_), channel_id=1, source_target_pairs={{0,8},{1,9},{2,10},{3,11},{4,12},{5,13},{6,14},{7,15},{8,0},{9,1},... | collective-permute-start | bytes 786440 | tf_op jit(solution)/shard_map/ppermute | solution.py:26
  43.7 1.5 %collective-permute-start.16 = (f32[4,64,256]{2,1,0:T(8,128)S(1)}, f32[4,64,256]{2,1,0:T(8,128)S(1)}, u32[]{:S(2)}, u32[]{:S(2)}) collective-permute-start(f32[4,64,256]{2,1,0:T(8,128)S(1)} %collective-permute-done.12.refs_2_), channel_id=1, source_target_pairs={{0,8},{1,9},{2,10},{3,11},{4,12},{5,13},{6,14},{7,15},{8,0},{9,1},... | collective-permute-start | bytes 786440 | tf_op jit(solution)/shard_map/ppermute | solution.py:26
  43.8 1.8 %collective-permute-start.15 = (f32[4,64,256]{2,1,0:T(8,128)S(1)}, f32[4,64,256]{2,1,0:T(8,128)S(1)}, u32[]{:S(2)}, u32[]{:S(2)}) collective-permute-start(f32[4,64,256]{2,1,0:T(8,128)S(1)} %collective-permute-done.8.refs_1_), channel_id=1, source_target_pairs={{0,8},{1,9},{2,10},{3,11},{4,12},{5,13},{6,14},{7,15},{8,0},{9,1},... | collective-permute-start | bytes 786440 | tf_op jit(solution)/shard_map/ppermute | solution.py:26
  44.2 1.4 %copy-start.3 = (f32[1024]{0:T(1024)S(1)}, f32[1024]{0:T(1024)}, u32[]{:S(2)}) copy-start(f32[1024]{0:T(1024)} %param.5) | copy-start | bytes 12292
  45.6 0.9 %copy-start.2 = (f32[2,64,256]{2,1,0:T(8,128)S(1)}, f32[2,64,256]{2,1,0:T(8,128)}, u32[]{:S(2)}) copy-start(f32[2,64,256]{2,1,0:T(8,128)} %copy-done.1) | copy-start | bytes 393220

commit v5 on v4

--- a/solution.py
+++ b/solution.py
@@ -76,17 +76,23 @@
 
 
 def times(a, b):
-    return lax.dot_general(a, b, (((0,), (0,)), ((), ())), preferred_element_type=jnp.float32)
+    return jnp.dot(a, b, preferred_element_type=jnp.float32)
 
 
-def product(place_ref, rows0_ref, rows1_ref, rows2_ref, rows3_ref, accum_ref, scale_ref, *refs):
+def order_rows(place_ref, *refs):
+    held, (high_ref, low_ref) = refs[:X], refs[X:]
+    at = lax.rem(place_ref[0] + place_ref[1], 2)
+    high, low = split(jnp.concatenate([ref[at] for ref in held] + [ref[1 - at] for ref in held], axis=0).T)
+    high_ref[...] = high
+    low_ref[...] = low
+
+
+def product(place_ref, high_ref, low_ref, accum_ref, scale_ref, *refs):
     packs, (scaled_ref, sums_ref) = (refs[:4], refs[4:8]), refs[8:]
-    yh, z, core, yl = (place_ref[i] for i in range(4))
-    at = lax.rem(yh + yl, 2)
-    held = (rows0_ref, rows1_ref, rows2_ref, rows3_ref)
-    high, low = split(jnp.concatenate([ref[at] for ref in held] + [ref[1 - at] for ref in held], axis=0))
-    depth = high.shape[0]
-    rows, width = rows0_ref.shape[2], refs[0].shape[2]
+    z, core = place_ref[0], place_ref[1]
+    high, low = high_ref[...], low_ref[...]
+    rows, depth = high.shape
+    width = refs[0].shape[2]
     squares = jnp.zeros((rows, 128), jnp.float32)
     for odd in range(2):
         for beside in range(CORE):
@@ -142,7 +148,8 @@
     groups = YL * X
 
     held = [send(block, along_z(2 * step)) for step in range(X)]
-    beside_yl = send(block, along_yl)
+    source, held[3] = lax.optimization_barrier((block, held[3]))
+    beside_yl = send(source, along_yl)
     planes = call(
         sort_planes,
         (f32(depth, rows),) * X,
@@ -157,15 +164,16 @@
     other_y = send(kept, along_y)
     passed = send(kept, pass_on)
     both_passed = send(kept, diagonal)
-    other_y, *from_x = lax.optimization_barrier((other_y, *from_x))
-    full_rows = [pair, *from_x]
+    low_type = jax.ShapeDtypeStruct((rows, groups * depth), jnp.bfloat16)
+    high, low = call(order_rows, (low_type, low_type), [place("yh", "yl"), pair, *from_x], flops=0)
+    other_y, high = lax.optimization_barrier((other_y, high))
     mine = [kept, other_y, passed, both_passed]
     others = [send(pack, across) for pack in mine]
 
     scaled, sums = call(
         product,
         (f32(rows, cols), f32(groups, 8, rows)),
-        [place("yh", "z", "core", "yl"), *full_rows, accum, col_scale[None], *mine, *others],
+        [place("z", "core"), high, low, accum, col_scale[None], *mine, *others],
         flops=6 * rows * cols * depth * groups,
     )
     sums = lax.all_to_all(sums, COL, 0, 0)

time: 58.6 us -> 58.4 us (level)
  local copies, waits for them, and re-layouts: 1.57 us -> 0.01 us
  Pallas kernels: 3.4 us -> 4.52 us
    unnamed x8 -> x4, local copies, waits for them, and re-layouts: 1.57 us -> 0.01 us
    pallas_call x3 -> x4, Pallas kernels: 3.4 us -> 4.52 us  [call(): pl.pallas_call(kernel, out_shape=out_shape, in_specs=[SMEM] * scalars + [...]
  transfers between devices with their start and end apart: 18 -> 18, of which waited for: 5 -> 5; matrix products, arithmetic and copies ran while one was open for 2% -> 2% of each run, Pallas kernels for 1% -> 2%
where the time goes in v5:
time: 58.4 us; the launch traced here: 58.2 us
  starting transfers between devices  37.4 us (64%)
  blocking collectives  9.01 us (15%)
  waiting for transfers between devices  6.08 us (10%)
  Pallas kernels  4.52 us (8%)
  other arithmetic  1.09 us (2%)
    ppermute x18, starting transfers between devices, send(): return lax.ppermute(value, ALL, pairs)  37.4 us
    all_to_all x1, blocking collectives, per_device(): sums = lax.all_to_all(sums, COL, 0, 0)  9.01 us
    ppermute x18, waiting for transfers between devices, send(): return lax.ppermute(value, ALL, pairs)  6.08 us
    pallas_call x4, Pallas kernels, call(): pl.pallas_call(kernel, out_shape=out_shape, in_specs=[SMEM] * scalars + [...  4.52 us
  transfers between devices with their start and end apart: 18, of which 5 were waited for; matrix products, arithmetic and copies ran while one was open for 2% of the time, Pallas kernels for 2%

profile of v5, /device:TPU:1, one launch (start us, length us, event | category | flops | bytes accessed | tf_op | source)
XLA Modules:
  0.0 58.2 jit_solution(8534083734567532133)
XLA Ops:
  0.0 6.8 %collective-permute-start.3 = (f32[64,256]{1,0:T(8,128)}, f32[64,256]{1,0:T(8,128)S(1)}, u32[]{:S(2)}, u32[]{:S(2)}) collective-permute-start(f32[64,256]{1,0:T(8,128)} %bitcast.16), channel_id=1, source_target_pairs={{0,96},{1,97},{2,98},{3,99},{4,224},{5,225},{6,226},{7,227},{8,104... | collective-permute-start | bytes 196616 | tf_op jit(solution)/shard_map/ppermute | solution.py:26
  6.9 1.0 %collective-permute-start.2 = (f32[64,256]{1,0:T(8,128)}, f32[64,256]{1,0:T(8,128)S(1)}, u32[]{:S(2)}, u32[]{:S(2)}) collective-permute-start(f32[64,256]{1,0:T(8,128)} %bitcast.17), channel_id=1, source_target_pairs={{0,64},{1,65},{2,66},{3,67},{4,192},{5,193},{6,194},{7,195},{8,72}... | collective-permute-start | bytes 196616 | tf_op jit(solution)/shard_map/ppermute | solution.py:26
  7.8 2.3 %collective-permute-start.1 = (f32[64,256]{1,0:T(8,128)}, f32[64,256]{1,0:T(8,128)S(1)}, u32[]{:S(2)}, u32[]{:S(2)}) collective-permute-start(f32[64,256]{1,0:T(8,128)} %bitcast.18), channel_id=1, source_target_pairs={{0,32},{1,33},{2,34},{3,35},{4,160},{5,161},{6,162},{7,163},{8,40}... | collective-permute-start | bytes 196616 | tf_op jit(solution)/shard_map/ppermute | solution.py:26
  10.1 1.5 %collective-permute-start = (f32[64,256]{1,0:T(8,128)}, f32[64,256]{1,0:T(8,128)S(1)}, u32[]{:S(2)}, u32[]{:S(2)}) collective-permute-start(f32[64,256]{1,0:T(8,128)} %bitcast.19), channel_id=1, source_target_pairs={{0,0},{1,1},{2,2},{3,3},{4,128},{5,129},{6,130},{7,131},{8,8},{9,9... | collective-permute-start | bytes 196616 | tf_op jit(solution)/shard_map/ppermute | solution.py:26
  11.6 3.9 %collective-permute-start.8 = (f32[64,256]{1,0:T(8,128)}, f32[64,256]{1,0:T(8,128)S(1)}, u32[]{:S(2)}, u32[]{:S(2)}) collective-permute-start(f32[64,256]{1,0:T(8,128)} %bitcast.20), channel_id=1, source_target_pairs={{0,4},{1,5},{2,6},{3,7},{4,0},{5,1},{6,2},{7,3},{8,12},{9,13},{10,... | collective-permute-start | bytes 196616 | tf_op jit(solution)/shard_map/ppermute | solution.py:26
  15.5 0.1 pad_add_fusion.1.place_ref
  15.6 0.6 %shard_map.37 = (f32[64,256]{1,0:T(8,128)S(1)}, f32[64,256]{1,0:T(8,128)S(1)}, f32[64,256]{1,0:T(8,128)S(1)}, f32[64,256]{1,0:T(8,128)S(1)}) custom-call(s32[2]{0:T(128)S(1)} %pad_add_fusion.1.place_ref, f32[64,256]{1,0:T(8,128)S(1)} %collective-permute-done.refs_0_, f32[64,256]{1,0:T(8,128)S(1)} %collective-permute-done.1.refs_1_, ...), custom_call_target="tpu_custom_call" | custom-call | bytes 2097152 | tf_op jit(solution)/shard_map/pallas_call | solution.py:125
  16.2 2.8 %collective-permute-start.5 = (f32[64,256]{1,0:T(8,128)S(1)}, f32[64,256]{1,0:T(8,128)S(1)}, u32[]{:S(2)}, u32[]{:S(2)}) collective-permute-start(f32[64,256]{1,0:T(8,128)S(1)} %get-tuple-element.21), channel_id=1, source_target_pairs={{0,2},{1,3},{2,0},{3,1},{4,6},{5,7},{6,4},{7,5},{8,10},{9,11},{10,... | collective-permute-start | bytes 196616 | tf_op jit(solution)/shard_map/ppermute | solution.py:26
  19.0 0.9 %collective-permute-start.6 = (f32[64,256]{1,0:T(8,128)S(1)}, f32[64,256]{1,0:T(8,128)S(1)}, u32[]{:S(2)}, u32[]{:S(2)}) collective-permute-start(f32[64,256]{1,0:T(8,128)S(1)} %get-tuple-element.22), channel_id=1, source_target_pairs={{0,3},{1,0},{2,1},{3,2},{4,7},{5,4},{6,5},{7,6},{8,11},{9,8},{10,9... | collective-permute-start | bytes 196616 | tf_op jit(solution)/shard_map/ppermute | solution.py:26
  19.9 0.6 %collective-permute-start.4 = (f32[64,256]{1,0:T(8,128)S(1)}, f32[64,256]{1,0:T(8,128)S(1)}, u32[]{:S(2)}, u32[]{:S(2)}) collective-permute-start(f32[64,256]{1,0:T(8,128)S(1)} %get-tuple-element.20), channel_id=1, source_target_pairs={{0,1},{1,2},{2,3},{3,0},{4,5},{5,6},{6,7},{7,4},{8,9},{9,10},{10,1... | collective-permute-start | bytes 196616 | tf_op jit(solution)/shard_map/ppermute | solution.py:26
  20.5 0.8 %pad_maximum_fusion.1.refs_0_ = f32[2,64,256]{2,1,0:T(8,128)S(1)} fusion(f32[1,64,256]{2,1,0:T(8,128)S(1)} %bitcast.22, f32[1,64,256]{2,1,0:T(8,128)} %bitcast.21), kind=kLoop, calls=%fused_computation.1 | loop fusion | flops 32768 | bytes 262144 | tf_op jit(solution)/shard_map/stack | solution.py:162
  21.3 2.1 %collective-permute-start.11 = (f32[2,64,256]{2,1,0:T(8,128)S(1)}, f32[2,64,256]{2,1,0:T(8,128)S(1)}, u32[]{:S(2)}, u32[]{:S(2)}) collective-permute-start(f32[2,64,256]{2,1,0:T(8,128)S(1)} %pad_maximum_fusion.1.refs_0_), channel_id=1, source_target_pairs={{0,3},{1,0},{2,1},{3,2},{4,7},{5,4},{6,5},{7,6},{8,11},{9,8},{10,9... | collective-permute-start | bytes 393224 | tf_op jit(solution)/shard_map/ppermute | solution.py:26
  23.5 0.7 %collective-permute-done.4 = f32[64,256]{1,0:T(8,128)S(1)} collective-permute-done((f32[64,256]{1,0:T(8,128)S(1)}, f32[64,256]{1,0:T(8,128)S(1)}, u32[]{:S(2)}, u32[]{:S(2)}) %collective-permute-start.4) | collective-permute-done | bytes 65568 | tf_op jit(solution)/shard_map/ppermute | solution.py:26
  24.2 5.5 %collective-permute-start.7 = (f32[4,64,256]{2,1,0:T(8,128)S(1)}, f32[4,64,256]{2,1,0:T(8,128)S(1)}, u32[]{:S(2)}, u32[]{:S(2)}) collective-permute-start(f32[4,64,256]{2,1,0:T(8,128)S(1)} %pad_maximum_fusion.refs_0_), channel_id=1, source_target_pairs={{0,128},{1,129},{2,130},{3,131},{4,132},{5,133},{6,134},{7,135},{8... | collective-permute-start | bytes 786440 | tf_op jit(solution)/shard_map/ppermute | solution.py:26
  29.7 1.2 %collective-permute-start.13 = (f32[4,64,256]{2,1,0:T(8,128)S(1)}, f32[4,64,256]{2,1,0:T(8,128)S(1)}, u32[]{:S(2)}, u32[]{:S(2)}) collective-permute-start(f32[4,64,256]{2,1,0:T(8,128)S(1)} %pad_maximum_fusion.refs_0_), channel_id=1, source_target_pairs={{0,144},{1,145},{2,146},{3,147},{4,148},{5,149},{6,150},{7,151},{8... | collective-permute-start | bytes 786440 | tf_op jit(solution)/shard_map/ppermute | solution.py:26
  30.9 1.4 %collective-permute-start.12 = (f32[4,64,256]{2,1,0:T(8,128)S(1)}, f32[4,64,256]{2,1,0:T(8,128)S(1)}, u32[]{:S(2)}, u32[]{:S(2)}) collective-permute-start(f32[4,64,256]{2,1,0:T(8,128)S(1)} %pad_maximum_fusion.refs_0_), channel_id=1, source_target_pairs={{0,16},{1,17},{2,18},{3,19},{4,20},{5,21},{6,22},{7,23},{8,120},{9... | collective-permute-start | bytes 786440 | tf_op jit(solution)/shard_map/ppermute | solution.py:26
  32.3 1.0 %collective-permute-start.10 = (f32[2,64,256]{2,1,0:T(8,128)S(1)}, f32[2,64,256]{2,1,0:T(8,128)S(1)}, u32[]{:S(2)}, u32[]{:S(2)}) collective-permute-start(f32[2,64,256]{2,1,0:T(8,128)S(1)} %pad_maximum_fusion.1.refs_0_), channel_id=1, source_target_pairs={{0,2},{1,3},{2,0},{3,1},{4,6},{5,7},{6,4},{7,5},{8,10},{9,11},{10,... | collective-permute-start | bytes 393224 | tf_op jit(solution)/shard_map/ppermute | solution.py:26
  33.2 0.7 %collective-permute-start.9 = (f32[2,64,256]{2,1,0:T(8,128)S(1)}, f32[2,64,256]{2,1,0:T(8,128)S(1)}, u32[]{:S(2)}, u32[]{:S(2)}) collective-permute-start(f32[2,64,256]{2,1,0:T(8,128)S(1)} %pad_maximum_fusion.1.refs_0_), channel_id=1, source_target_pairs={{0,1},{1,2},{2,3},{3,0},{4,5},{5,6},{6,7},{7,4},{8,9},{9,10},{10,1... | collective-permute-start | bytes 393224 | tf_op jit(solution)/shard_map/ppermute | solution.py:26
  33.9 0.1 pad_add_fusion.2.place_ref
  34.0 3.9 %collective-permute-done.10.refs_2_ = f32[2,64,256]{2,1,0:T(8,128)S(1)} collective-permute-done((f32[2,64,256]{2,1,0:T(8,128)S(1)}, f32[2,64,256]{2,1,0:T(8,128)S(1)}, u32[]{:S(2)}, u32[]{:S(2)}) %collective-permute-start.10) | collective-permute-done | bytes 131104 | tf_op jit(solution)/shard_map/ppermute | solution.py:26
  37.9 3.9 %collective-permute-start.14 = (f32[4,64,256]{2,1,0:T(8,128)S(1)}, f32[4,64,256]{2,1,0:T(8,128)S(1)}, u32[]{:S(2)}, u32[]{:S(2)}) collective-permute-start(f32[4,64,256]{2,1,0:T(8,128)S(1)} %pad_maximum_fusion.refs_0_), channel_id=1, source_target_pairs={{0,8},{1,9},{2,10},{3,11},{4,12},{5,13},{6,14},{7,15},{8,0},{9,1},... | collective-permute-start | bytes 786440 | tf_op jit(solution)/shard_map/ppermute | solution.py:26
  41.8 0.8 %shard_map.38 = (bf16[256,512]{1,0:T(8,128)(2,1)S(1)}, bf16[256,512]{1,0:T(8,128)(2,1)S(1)}) custom-call(s32[2]{0:T(128)S(1)} %pad_add_fusion.2.place_ref, f32[2,64,256]{2,1,0:T(8,128)S(1)} %pad_maximum_fusion.1.refs_0_, f32[2,64,256]{2,1,0:T(8,128)S(1)} %collective-permute-done.9.refs_1_, f32[2,64,256]{2,1,0:T(8,128)S(1)} %collective-permute-done.10.refs_2_, ...), custom_call_target="tpu_custom_call" | custom-call | bytes 2097152 | tf_op jit(solution)/shard_map/pallas_call | solution.py:125
  42.5 1.4 %collective-permute-start.17 = (f32[4,64,256]{2,1,0:T(8,128)S(1)}, f32[4,64,256]{2,1,0:T(8,128)S(1)}, u32[]{:S(2)}, u32[]{:S(2)}) collective-permute-start(f32[4,64,256]{2,1,0:T(8,128)S(1)} %collective-permute-done.13.refs_3_), channel_id=1, source_target_pairs={{0,8},{1,9},{2,10},{3,11},{4,12},{5,13},{6,14},{7,15},{8,0},{9,1},... | collective-permute-start | bytes 786440 | tf_op jit(solution)/shard_map/ppermute | solution.py:26
  43.9 0.1 collective-permute-start.16
  44.0 0.4 collective-permute-start.15
  44.4 0.1 pad_add_fusion.place_ref
  44.5 0.6 collective-permute-done.17.refs_7_
  45.1 0.4 collective-permute-done.16.refs_6_
  45.5 0.5 collective-permute-done.15.refs_5_
  46.0 2.1 %shard_map.39 = (f32[256,1024]{1,0:T(8,128)S(1)}, f32[8,8,256]{2,1,0:T(8,128)S(1)}) custom-call(s32[2]{0:T(128)S(1)} %pad_add_fusion.place_ref, bf16[256,512]{1,0:T(8,128)(2,1)S(1)} %get-tuple-element.26.high_ref, bf16[256,512]{1,0:T(8,128)(2,1)S(1)} %get-tuple-element.27.low_ref, f32[256,1024]{1,0:T(8,128)S(1)} %copy-done, f32[1,1024]{1,0:T(1,128)S(1)} %bitcast.15, ...), custom_call_target="tpu_custom_call" | custom-call | flops 805306368 | bytes 2097152 | tf_op jit(solution)/shard_map/pallas_call | solution.py:125
  48.0 9.0 %all_to_all.5.sums_ref = f32[8,8,256]{2,1,0:T(8,128)S(1)} all-to-all(f32[8,8,256]{2,1,0:T(8,128)S(1)} %get-tuple-element.30), channel_id=1, replica_groups=mesh['yh'=2,'z'=8,'core'=2,'yl'=2,'x'=4] {'yl','x'}, dimensions={0} | all-to-all | bytes 131072 | tf_op jit(solution)/shard_map/all_to_all | solution.py:179
  57.0 1.1 %shard_map.40 = f32[256,1024]{1,0:T(8,128)} custom-call(f32[256,1024]{1,0:T(8,128)S(1)} %get-tuple-element.29.scaled_ref, f32[8,8,256]{2,1,0:T(8,128)S(1)} %all_to_all.5.sums_ref), custom_call_target="tpu_custom_call" | custom-call | bytes 2097152 | tf_op jit(solution)/shard_map/pallas_call | solution.py:125
  (18 shorter events, 0.1 us)
Async XLA Ops:
  0.0 46.0 %copy-start = (f32[256,1024]{1,0:T(8,128)S(1)}, f32[256,1024]{1,0:T(8,128)}, u32[]{:S(2)}) copy-start(f32[256,1024]{1,0:T(8,128)} %accum_ref.1) | copy-start | bytes 3145732
  0.0 11.6 %collective-permute-start.3 = (f32[64,256]{1,0:T(8,128)}, f32[64,256]{1,0:T(8,128)S(1)}, u32[]{:S(2)}, u32[]{:S(2)}) collective-permute-start(f32[64,256]{1,0:T(8,128)} %bitcast.16), channel_id=1, source_target_pairs={{0,96},{1,97},{2,98},{3,99},{4,224},{5,225},{6,226},{7,227},{8,104... | collective-permute-start | bytes 196616 | tf_op jit(solution)/shard_map/ppermute | solution.py:26
  6.9 8.7 %collective-permute-start.2 = (f32[64,256]{1,0:T(8,128)}, f32[64,256]{1,0:T(8,128)S(1)}, u32[]{:S(2)}, u32[]{:S(2)}) collective-permute-start(f32[64,256]{1,0:T(8,128)} %bitcast.17), channel_id=1, source_target_pairs={{0,64},{1,65},{2,66},{3,67},{4,192},{5,193},{6,194},{7,195},{8,72}... | collective-permute-start | bytes 196616 | tf_op jit(solution)/shard_map/ppermute | solution.py:26
  7.8 7.8 %collective-permute-start.1 = (f32[64,256]{1,0:T(8,128)}, f32[64,256]{1,0:T(8,128)S(1)}, u32[]{:S(2)}, u32[]{:S(2)}) collective-permute-start(f32[64,256]{1,0:T(8,128)} %bitcast.18), channel_id=1, source_target_pairs={{0,32},{1,33},{2,34},{3,35},{4,160},{5,161},{6,162},{7,163},{8,40}... | collective-permute-start | bytes 196616 | tf_op jit(solution)/shard_map/ppermute | solution.py:26
  10.1 5.5 %collective-permute-start = (f32[64,256]{1,0:T(8,128)}, f32[64,256]{1,0:T(8,128)S(1)}, u32[]{:S(2)}, u32[]{:S(2)}) collective-permute-start(f32[64,256]{1,0:T(8,128)} %bitcast.19), channel_id=1, source_target_pairs={{0,0},{1,1},{2,2},{3,3},{4,128},{5,129},{6,130},{7,131},{8,8},{9,9... | collective-permute-start | bytes 196616 | tf_op jit(solution)/shard_map/ppermute | solution.py:26
  11.6 8.9 %collective-permute-start.8 = (f32[64,256]{1,0:T(8,128)}, f32[64,256]{1,0:T(8,128)S(1)}, u32[]{:S(2)}, u32[]{:S(2)}) collective-permute-start(f32[64,256]{1,0:T(8,128)} %bitcast.20), channel_id=1, source_target_pairs={{0,4},{1,5},{2,6},{3,7},{4,0},{5,1},{6,2},{7,3},{8,12},{9,13},{10,... | collective-permute-start | bytes 196616 | tf_op jit(solution)/shard_map/ppermute | solution.py:26
  16.2 7.3 %collective-permute-start.5 = (f32[64,256]{1,0:T(8,128)S(1)}, f32[64,256]{1,0:T(8,128)S(1)}, u32[]{:S(2)}, u32[]{:S(2)}) collective-permute-start(f32[64,256]{1,0:T(8,128)S(1)} %get-tuple-element.21), channel_id=1, source_target_pairs={{0,2},{1,3},{2,0},{3,1},{4,6},{5,7},{6,4},{7,5},{8,10},{9,11},{10,... | collective-permute-start | bytes 196616 | tf_op jit(solution)/shard_map/ppermute | solution.py:26
  19.0 4.5 %collective-permute-start.6 = (f32[64,256]{1,0:T(8,128)S(1)}, f32[64,256]{1,0:T(8,128)S(1)}, u32[]{:S(2)}, u32[]{:S(2)}) collective-permute-start(f32[64,256]{1,0:T(8,128)S(1)} %get-tuple-element.22), channel_id=1, source_target_pairs={{0,3},{1,0},{2,1},{3,2},{4,7},{5,4},{6,5},{7,6},{8,11},{9,8},{10,9... | collective-permute-start | bytes 196616 | tf_op jit(solution)/shard_map/ppermute | solution.py:26
  19.9 4.3 %collective-permute-start.4 = (f32[64,256]{1,0:T(8,128)S(1)}, f32[64,256]{1,0:T(8,128)S(1)}, u32[]{:S(2)}, u32[]{:S(2)}) collective-permute-start(f32[64,256]{1,0:T(8,128)S(1)} %get-tuple-element.20), channel_id=1, source_target_pairs={{0,1},{1,2},{2,3},{3,0},{4,5},{5,6},{6,7},{7,4},{8,9},{9,10},{10,1... | collective-permute-start | bytes 196616 | tf_op jit(solution)/shard_map/ppermute | solution.py:26
  21.3 11.9 %collective-permute-start.11 = (f32[2,64,256]{2,1,0:T(8,128)S(1)}, f32[2,64,256]{2,1,0:T(8,128)S(1)}, u32[]{:S(2)}, u32[]{:S(2)}) collective-permute-start(f32[2,64,256]{2,1,0:T(8,128)S(1)} %pad_maximum_fusion.1.refs_0_), channel_id=1, source_target_pairs={{0,3},{1,0},{2,1},{3,2},{4,7},{5,4},{6,5},{7,6},{8,11},{9,8},{10,9... | collective-permute-start | bytes 393224 | tf_op jit(solution)/shard_map/ppermute | solution.py:26
  24.2 18.3 %collective-permute-start.7 = (f32[4,64,256]{2,1,0:T(8,128)S(1)}, f32[4,64,256]{2,1,0:T(8,128)S(1)}, u32[]{:S(2)}, u32[]{:S(2)}) collective-permute-start(f32[4,64,256]{2,1,0:T(8,128)S(1)} %pad_maximum_fusion.refs_0_), channel_id=1, source_target_pairs={{0,128},{1,129},{2,130},{3,131},{4,132},{5,133},{6,134},{7,135},{8... | collective-permute-start | bytes 786440 | tf_op jit(solution)/shard_map/ppermute | solution.py:26
  29.7 12.8 %collective-permute-start.13 = (f32[4,64,256]{2,1,0:T(8,128)S(1)}, f32[4,64,256]{2,1,0:T(8,128)S(1)}, u32[]{:S(2)}, u32[]{:S(2)}) collective-permute-start(f32[4,64,256]{2,1,0:T(8,128)S(1)} %pad_maximum_fusion.refs_0_), channel_id=1, source_target_pairs={{0,144},{1,145},{2,146},{3,147},{4,148},{5,149},{6,150},{7,151},{8... | collective-permute-start | bytes 786440 | tf_op jit(solution)/shard_map/ppermute | solution.py:26
  30.9 13.0 %collective-permute-start.12 = (f32[4,64,256]{2,1,0:T(8,128)S(1)}, f32[4,64,256]{2,1,0:T(8,128)S(1)}, u32[]{:S(2)}, u32[]{:S(2)}) collective-permute-start(f32[4,64,256]{2,1,0:T(8,128)S(1)} %pad_maximum_fusion.refs_0_), channel_id=1, source_target_pairs={{0,16},{1,17},{2,18},{3,19},{4,20},{5,21},{6,22},{7,23},{8,120},{9... | collective-permute-start | bytes 786440 | tf_op jit(solution)/shard_map/ppermute | solution.py:26
  32.3 5.6 %collective-permute-start.10 = (f32[2,64,256]{2,1,0:T(8,128)S(1)}, f32[2,64,256]{2,1,0:T(8,128)S(1)}, u32[]{:S(2)}, u32[]{:S(2)}) collective-permute-start(f32[2,64,256]{2,1,0:T(8,128)S(1)} %pad_maximum_fusion.1.refs_0_), channel_id=1, source_target_pairs={{0,2},{1,3},{2,0},{3,1},{4,6},{5,7},{6,4},{7,5},{8,10},{9,11},{10,... | collective-permute-start | bytes 393224 | tf_op jit(solution)/shard_map/ppermute | solution.py:26
  33.2 8.5 %collective-permute-start.9 = (f32[2,64,256]{2,1,0:T(8,128)S(1)}, f32[2,64,256]{2,1,0:T(8,128)S(1)}, u32[]{:S(2)}, u32[]{:S(2)}) collective-permute-start(f32[2,64,256]{2,1,0:T(8,128)S(1)} %pad_maximum_fusion.1.refs_0_), channel_id=1, source_target_pairs={{0,1},{1,2},{2,3},{3,0},{4,5},{5,6},{6,7},{7,4},{8,9},{9,10},{10,1... | collective-permute-start | bytes 393224 | tf_op jit(solution)/shard_map/ppermute | solution.py:26
  37.9 6.6 %collective-permute-start.14 = (f32[4,64,256]{2,1,0:T(8,128)S(1)}, f32[4,64,256]{2,1,0:T(8,128)S(1)}, u32[]{:S(2)}, u32[]{:S(2)}) collective-permute-start(f32[4,64,256]{2,1,0:T(8,128)S(1)} %pad_maximum_fusion.refs_0_), channel_id=1, source_target_pairs={{0,8},{1,9},{2,10},{3,11},{4,12},{5,13},{6,14},{7,15},{8,0},{9,1},... | collective-permute-start | bytes 786440 | tf_op jit(solution)/shard_map/ppermute | solution.py:26
  42.5 2.5 %collective-permute-start.17 = (f32[4,64,256]{2,1,0:T(8,128)S(1)}, f32[4,64,256]{2,1,0:T(8,128)S(1)}, u32[]{:S(2)}, u32[]{:S(2)}) collective-permute-start(f32[4,64,256]{2,1,0:T(8,128)S(1)} %collective-permute-done.13.refs_3_), channel_id=1, source_target_pairs={{0,8},{1,9},{2,10},{3,11},{4,12},{5,13},{6,14},{7,15},{8,0},{9,1},... | collective-permute-start | bytes 786440 | tf_op jit(solution)/shard_map/ppermute | solution.py:26
  43.9 1.5 %collective-permute-start.16 = (f32[4,64,256]{2,1,0:T(8,128)S(1)}, f32[4,64,256]{2,1,0:T(8,128)S(1)}, u32[]{:S(2)}, u32[]{:S(2)}) collective-permute-start(f32[4,64,256]{2,1,0:T(8,128)S(1)} %collective-permute-done.12.refs_2_), channel_id=1, source_target_pairs={{0,8},{1,9},{2,10},{3,11},{4,12},{5,13},{6,14},{7,15},{8,0},{9,1},... | collective-permute-start | bytes 786440 | tf_op jit(solution)/shard_map/ppermute | solution.py:26
  44.0 1.9 %collective-permute-start.15 = (f32[4,64,256]{2,1,0:T(8,128)S(1)}, f32[4,64,256]{2,1,0:T(8,128)}, u32[]{:S(2)}, u32[]{:S(2)}) collective-permute-start(f32[4,64,256]{2,1,0:T(8,128)S(1)} %collective-permute-done.7.refs_1_), channel_id=1, source_target_pairs={{0,8},{1,9},{2,10},{3,11},{4,12},{5,13},{6,14},{7,15},{8,0},{9,1},... | collective-permute-start | bytes 786440 | tf_op jit(solution)/shard_map/ppermute | solution.py:26
  44.4 1.5 %copy-start.1 = (f32[1024]{0:T(1024)S(1)}, f32[1024]{0:T(1024)}, u32[]{:S(2)}) copy-start(f32[1024]{0:T(1024)} %param.5) | copy-start | bytes 12292

commit v6 on v5

--- a/solution.py
+++ b/solution.py
@@ -166,7 +166,7 @@
     both_passed = send(kept, diagonal)
     low_type = jax.ShapeDtypeStruct((rows, groups * depth), jnp.bfloat16)
     high, low = call(order_rows, (low_type, low_type), [place("yh", "yl"), pair, *from_x], flops=0)
-    other_y, high = lax.optimization_barrier((other_y, high))
+    both_passed, high = lax.optimization_barrier((both_passed, high))
     mine = [kept, other_y, passed, both_passed]
     others = [send(pack, across) for pack in mine]
 

time: 58.4 us -> 58.4 us (level)
  no operation moved by 1% of the time
where the time goes in v6:
time: 58.4 us; the launch traced here: 58.1 us
  starting transfers between devices  37.3 us (64%)
  blocking collectives  9.09 us (16%)
  waiting for transfers between devices  6.08 us (10%)
  Pallas kernels  4.52 us (8%)
  other arithmetic  1.09 us (2%)
    ppermute x18, starting transfers between devices, send(): return lax.ppermute(value, ALL, pairs)  37.3 us
    all_to_all x1, blocking collectives, per_device(): sums = lax.all_to_all(sums, COL, 0, 0)  9.09 us
    ppermute x18, waiting for transfers between devices, send(): return lax.ppermute(value, ALL, pairs)  6.08 us
    pallas_call x4, Pallas kernels, call(): pl.pallas_call(kernel, out_shape=out_shape, in_specs=[SMEM] * scalars + [...  4.52 us
  transfers between devices with their start and end apart: 18, of which 5 were waited for; matrix products, arithmetic and copies ran while one was open for 2% of the time, Pallas kernels for 2%

profile of v6, /device:TPU:1, one launch (start us, length us, event | category | flops | bytes accessed | tf_op | source)
XLA Modules:
  0.0 58.1 jit_solution(17268720403924398861)
XLA Ops:
  0.0 6.8 %collective-permute-start.3 = (f32[64,256]{1,0:T(8,128)}, f32[64,256]{1,0:T(8,128)S(1)}, u32[]{:S(2)}, u32[]{:S(2)}) collective-permute-start(f32[64,256]{1,0:T(8,128)} %bitcast.16), channel_id=1, source_target_pairs={{0,96},{1,97},{2,98},{3,99},{4,224},{5,225},{6,226},{7,227},{8,104... | collective-permute-start | bytes 196616 | tf_op jit(solution)/shard_map/ppermute | solution.py:26
  6.9 1.0 %collective-permute-start.2 = (f32[64,256]{1,0:T(8,128)}, f32[64,256]{1,0:T(8,128)S(1)}, u32[]{:S(2)}, u32[]{:S(2)}) collective-permute-start(f32[64,256]{1,0:T(8,128)} %bitcast.17), channel_id=1, source_target_pairs={{0,64},{1,65},{2,66},{3,67},{4,192},{5,193},{6,194},{7,195},{8,72}... | collective-permute-start | bytes 196616 | tf_op jit(solution)/shard_map/ppermute | solution.py:26
  7.8 2.3 %collective-permute-start.1 = (f32[64,256]{1,0:T(8,128)}, f32[64,256]{1,0:T(8,128)S(1)}, u32[]{:S(2)}, u32[]{:S(2)}) collective-permute-start(f32[64,256]{1,0:T(8,128)} %bitcast.18), channel_id=1, source_target_pairs={{0,32},{1,33},{2,34},{3,35},{4,160},{5,161},{6,162},{7,163},{8,40}... | collective-permute-start | bytes 196616 | tf_op jit(solution)/shard_map/ppermute | solution.py:26
  10.1 1.5 %collective-permute-start = (f32[64,256]{1,0:T(8,128)}, f32[64,256]{1,0:T(8,128)S(1)}, u32[]{:S(2)}, u32[]{:S(2)}) collective-permute-start(f32[64,256]{1,0:T(8,128)} %bitcast.19), channel_id=1, source_target_pairs={{0,0},{1,1},{2,2},{3,3},{4,128},{5,129},{6,130},{7,131},{8,8},{9,9... | collective-permute-start | bytes 196616 | tf_op jit(solution)/shard_map/ppermute | solution.py:26
  11.6 0.0 collective-permute-done.3.refs_3_
  11.6 3.9 %collective-permute-start.8 = (f32[64,256]{1,0:T(8,128)}, f32[64,256]{1,0:T(8,128)S(1)}, u32[]{:S(2)}, u32[]{:S(2)}) collective-permute-start(f32[64,256]{1,0:T(8,128)} %bitcast.20), channel_id=1, source_target_pairs={{0,4},{1,5},{2,6},{3,7},{4,0},{5,1},{6,2},{7,3},{8,12},{9,13},{10,... | collective-permute-start | bytes 196616 | tf_op jit(solution)/shard_map/ppermute | solution.py:26
  15.5 0.1 pad_add_fusion.1.place_ref
  15.6 0.6 %shard_map.37 = (f32[64,256]{1,0:T(8,128)S(1)}, f32[64,256]{1,0:T(8,128)S(1)}, f32[64,256]{1,0:T(8,128)S(1)}, f32[64,256]{1,0:T(8,128)S(1)}) custom-call(s32[2]{0:T(128)S(1)} %pad_add_fusion.1.place_ref, f32[64,256]{1,0:T(8,128)S(1)} %collective-permute-done.refs_0_, f32[64,256]{1,0:T(8,128)S(1)} %collective-permute-done.1.refs_1_, ...), custom_call_target="tpu_custom_call" | custom-call | bytes 2097152 | tf_op jit(solution)/shard_map/pallas_call | solution.py:125
  16.2 2.8 %collective-permute-start.5 = (f32[64,256]{1,0:T(8,128)S(1)}, f32[64,256]{1,0:T(8,128)S(1)}, u32[]{:S(2)}, u32[]{:S(2)}) collective-permute-start(f32[64,256]{1,0:T(8,128)S(1)} %get-tuple-element.21), channel_id=1, source_target_pairs={{0,2},{1,3},{2,0},{3,1},{4,6},{5,7},{6,4},{7,5},{8,10},{9,11},{10,... | collective-permute-start | bytes 196616 | tf_op jit(solution)/shard_map/ppermute | solution.py:26
  19.0 0.9 %collective-permute-start.6 = (f32[64,256]{1,0:T(8,128)S(1)}, f32[64,256]{1,0:T(8,128)S(1)}, u32[]{:S(2)}, u32[]{:S(2)}) collective-permute-start(f32[64,256]{1,0:T(8,128)S(1)} %get-tuple-element.22), channel_id=1, source_target_pairs={{0,3},{1,0},{2,1},{3,2},{4,7},{5,4},{6,5},{7,6},{8,11},{9,8},{10,9... | collective-permute-start | bytes 196616 | tf_op jit(solution)/shard_map/ppermute | solution.py:26
  19.9 0.6 %collective-permute-start.4 = (f32[64,256]{1,0:T(8,128)S(1)}, f32[64,256]{1,0:T(8,128)S(1)}, u32[]{:S(2)}, u32[]{:S(2)}) collective-permute-start(f32[64,256]{1,0:T(8,128)S(1)} %get-tuple-element.20), channel_id=1, source_target_pairs={{0,1},{1,2},{2,3},{3,0},{4,5},{5,6},{6,7},{7,4},{8,9},{9,10},{10,1... | collective-permute-start | bytes 196616 | tf_op jit(solution)/shard_map/ppermute | solution.py:26
  20.5 0.8 %pad_maximum_fusion.1.refs_0_ = f32[2,64,256]{2,1,0:T(8,128)S(1)} fusion(f32[1,64,256]{2,1,0:T(8,128)S(1)} %bitcast.22, f32[1,64,256]{2,1,0:T(8,128)} %bitcast.21), kind=kLoop, calls=%fused_computation.1 | loop fusion | flops 32768 | bytes 262144 | tf_op jit(solution)/shard_map/stack | solution.py:162
  21.3 2.1 %collective-permute-start.11 = (f32[2,64,256]{2,1,0:T(8,128)S(1)}, f32[2,64,256]{2,1,0:T(8,128)S(1)}, u32[]{:S(2)}, u32[]{:S(2)}) collective-permute-start(f32[2,64,256]{2,1,0:T(8,128)S(1)} %pad_maximum_fusion.1.refs_0_), channel_id=1, source_target_pairs={{0,3},{1,0},{2,1},{3,2},{4,7},{5,4},{6,5},{7,6},{8,11},{9,8},{10,9... | collective-permute-start | bytes 393224 | tf_op jit(solution)/shard_map/ppermute | solution.py:26
  23.5 0.7 %collective-permute-done.4 = f32[64,256]{1,0:T(8,128)S(1)} collective-permute-done((f32[64,256]{1,0:T(8,128)S(1)}, f32[64,256]{1,0:T(8,128)S(1)}, u32[]{:S(2)}, u32[]{:S(2)}) %collective-permute-start.4) | collective-permute-done | bytes 65568 | tf_op jit(solution)/shard_map/ppermute | solution.py:26
  24.2 6.6 %collective-permute-start.7 = (f32[4,64,256]{2,1,0:T(8,128)S(1)}, f32[4,64,256]{2,1,0:T(8,128)S(1)}, u32[]{:S(2)}, u32[]{:S(2)}) collective-permute-start(f32[4,64,256]{2,1,0:T(8,128)S(1)} %pad_maximum_fusion.refs_0_), channel_id=1, source_target_pairs={{0,144},{1,145},{2,146},{3,147},{4,148},{5,149},{6,150},{7,151},{8... | collective-permute-start | bytes 786440 | tf_op jit(solution)/shard_map/ppermute | solution.py:26
  30.8 1.4 %collective-permute-start.13 = (f32[4,64,256]{2,1,0:T(8,128)S(1)}, f32[4,64,256]{2,1,0:T(8,128)S(1)}, u32[]{:S(2)}, u32[]{:S(2)}) collective-permute-start(f32[4,64,256]{2,1,0:T(8,128)S(1)} %pad_maximum_fusion.refs_0_), channel_id=1, source_target_pairs={{0,16},{1,17},{2,18},{3,19},{4,20},{5,21},{6,22},{7,23},{8,120},{9... | collective-permute-start | bytes 786440 | tf_op jit(solution)/shard_map/ppermute | solution.py:26
  32.2 1.0 %collective-permute-start.10 = (f32[2,64,256]{2,1,0:T(8,128)S(1)}, f32[2,64,256]{2,1,0:T(8,128)S(1)}, u32[]{:S(2)}, u32[]{:S(2)}) collective-permute-start(f32[2,64,256]{2,1,0:T(8,128)S(1)} %pad_maximum_fusion.1.refs_0_), channel_id=1, source_target_pairs={{0,2},{1,3},{2,0},{3,1},{4,6},{5,7},{6,4},{7,5},{8,10},{9,11},{10,... | collective-permute-start | bytes 393224 | tf_op jit(solution)/shard_map/ppermute | solution.py:26
  33.1 0.7 %collective-permute-start.9 = (f32[2,64,256]{2,1,0:T(8,128)S(1)}, f32[2,64,256]{2,1,0:T(8,128)S(1)}, u32[]{:S(2)}, u32[]{:S(2)}) collective-permute-start(f32[2,64,256]{2,1,0:T(8,128)S(1)} %pad_maximum_fusion.1.refs_0_), channel_id=1, source_target_pairs={{0,1},{1,2},{2,3},{3,0},{4,5},{5,6},{6,7},{7,4},{8,9},{9,10},{10,1... | collective-permute-start | bytes 393224 | tf_op jit(solution)/shard_map/ppermute | solution.py:26
  33.8 0.1 pad_add_fusion.2.place_ref
  33.9 3.9 %collective-permute-done.10.refs_2_ = f32[2,64,256]{2,1,0:T(8,128)S(1)} collective-permute-done((f32[2,64,256]{2,1,0:T(8,128)S(1)}, f32[2,64,256]{2,1,0:T(8,128)S(1)}, u32[]{:S(2)}, u32[]{:S(2)}) %collective-permute-start.10) | collective-permute-done | bytes 131104 | tf_op jit(solution)/shard_map/ppermute | solution.py:26
  37.8 3.9 %collective-permute-start.14 = (f32[4,64,256]{2,1,0:T(8,128)S(1)}, f32[4,64,256]{2,1,0:T(8,128)S(1)}, u32[]{:S(2)}, u32[]{:S(2)}) collective-permute-start(f32[4,64,256]{2,1,0:T(8,128)S(1)} %pad_maximum_fusion.refs_0_), channel_id=1, source_target_pairs={{0,8},{1,9},{2,10},{3,11},{4,12},{5,13},{6,14},{7,15},{8,0},{9,1},... | collective-permute-start | bytes 786440 | tf_op jit(solution)/shard_map/ppermute | solution.py:26
  41.7 0.8 %shard_map.38 = (bf16[256,512]{1,0:T(8,128)(2,1)S(1)}, bf16[256,512]{1,0:T(8,128)(2,1)S(1)}) custom-call(s32[2]{0:T(128)S(1)} %pad_add_fusion.2.place_ref, f32[2,64,256]{2,1,0:T(8,128)S(1)} %pad_maximum_fusion.1.refs_0_, f32[2,64,256]{2,1,0:T(8,128)S(1)} %collective-permute-done.9.refs_1_, f32[2,64,256]{2,1,0:T(8,128)S(1)} %collective-permute-done.10.refs_2_, ...), custom_call_target="tpu_custom_call" | custom-call | bytes 2097152 | tf_op jit(solution)/shard_map/pallas_call | solution.py:125
  42.4 1.4 %collective-permute-start.16 = (f32[4,64,256]{2,1,0:T(8,128)S(1)}, f32[4,64,256]{2,1,0:T(8,128)S(1)}, u32[]{:S(2)}, u32[]{:S(2)}) collective-permute-start(f32[4,64,256]{2,1,0:T(8,128)S(1)} %collective-permute-done.13.refs_2_), channel_id=1, source_target_pairs={{0,8},{1,9},{2,10},{3,11},{4,12},{5,13},{6,14},{7,15},{8,0},{9,1},... | collective-permute-start | bytes 786440 | tf_op jit(solution)/shard_map/ppermute | solution.py:26
  43.8 0.2 collective-permute-start.15
  44.0 0.3 collective-permute-start.17
  44.3 0.1 pad_add_fusion.place_ref
  44.4 0.6 collective-permute-done.16.refs_6_
  45.0 0.4 collective-permute-done.15.refs_5_
  45.4 0.5 collective-permute-done.17.refs_7_
  45.9 2.1 %shard_map.39 = (f32[256,1024]{1,0:T(8,128)S(1)}, f32[8,8,256]{2,1,0:T(8,128)S(1)}) custom-call(s32[2]{0:T(128)S(1)} %pad_add_fusion.place_ref, bf16[256,512]{1,0:T(8,128)(2,1)S(1)} %get-tuple-element.26.high_ref, bf16[256,512]{1,0:T(8,128)(2,1)S(1)} %get-tuple-element.27.low_ref, f32[256,1024]{1,0:T(8,128)S(1)} %copy-done, f32[1,1024]{1,0:T(1,128)S(1)} %bitcast.15, ...), custom_call_target="tpu_custom_call" | custom-call | flops 805306368 | bytes 2097152 | tf_op jit(solution)/shard_map/pallas_call | solution.py:125
  47.9 9.1 %all_to_all.5.sums_ref = f32[8,8,256]{2,1,0:T(8,128)S(1)} all-to-all(f32[8,8,256]{2,1,0:T(8,128)S(1)} %get-tuple-element.30), channel_id=1, replica_groups=mesh['yh'=2,'z'=8,'core'=2,'yl'=2,'x'=4] {'yl','x'}, dimensions={0} | all-to-all | bytes 131072 | tf_op jit(solution)/shard_map/all_to_all | solution.py:179
  57.0 1.1 %shard_map.40 = f32[256,1024]{1,0:T(8,128)} custom-call(f32[256,1024]{1,0:T(8,128)S(1)} %get-tuple-element.29.scaled_ref, f32[8,8,256]{2,1,0:T(8,128)S(1)} %all_to_all.5.sums_ref), custom_call_target="tpu_custom_call" | custom-call | bytes 2097152 | tf_op jit(solution)/shard_map/pallas_call | solution.py:125
  (18 shorter events, 0.1 us)
Async XLA Ops:
  0.0 45.9 %copy-start = (f32[256,1024]{1,0:T(8,128)S(1)}, f32[256,1024]{1,0:T(8,128)}, u32[]{:S(2)}) copy-start(f32[256,1024]{1,0:T(8,128)} %accum_ref.1) | copy-start | bytes 3145732
  0.0 11.6 %collective-permute-start.3 = (f32[64,256]{1,0:T(8,128)}, f32[64,256]{1,0:T(8,128)S(1)}, u32[]{:S(2)}, u32[]{:S(2)}) collective-permute-start(f32[64,256]{1,0:T(8,128)} %bitcast.16), channel_id=1, source_target_pairs={{0,96},{1,97},{2,98},{3,99},{4,224},{5,225},{6,226},{7,227},{8,104... | collective-permute-start | bytes 196616 | tf_op jit(solution)/shard_map/ppermute | solution.py:26
  6.9 8.7 %collective-permute-start.2 = (f32[64,256]{1,0:T(8,128)}, f32[64,256]{1,0:T(8,128)S(1)}, u32[]{:S(2)}, u32[]{:S(2)}) collective-permute-start(f32[64,256]{1,0:T(8,128)} %bitcast.17), channel_id=1, source_target_pairs={{0,64},{1,65},{2,66},{3,67},{4,192},{5,193},{6,194},{7,195},{8,72}... | collective-permute-start | bytes 196616 | tf_op jit(solution)/shard_map/ppermute | solution.py:26
  7.8 7.8 %collective-permute-start.1 = (f32[64,256]{1,0:T(8,128)}, f32[64,256]{1,0:T(8,128)S(1)}, u32[]{:S(2)}, u32[]{:S(2)}) collective-permute-start(f32[64,256]{1,0:T(8,128)} %bitcast.18), channel_id=1, source_target_pairs={{0,32},{1,33},{2,34},{3,35},{4,160},{5,161},{6,162},{7,163},{8,40}... | collective-permute-start | bytes 196616 | tf_op jit(solution)/shard_map/ppermute | solution.py:26
  10.1 5.5 %collective-permute-start = (f32[64,256]{1,0:T(8,128)}, f32[64,256]{1,0:T(8,128)S(1)}, u32[]{:S(2)}, u32[]{:S(2)}) collective-permute-start(f32[64,256]{1,0:T(8,128)} %bitcast.19), channel_id=1, source_target_pairs={{0,0},{1,1},{2,2},{3,3},{4,128},{5,129},{6,130},{7,131},{8,8},{9,9... | collective-permute-start | bytes 196616 | tf_op jit(solution)/shard_map/ppermute | solution.py:26
  11.6 8.9 %collective-permute-start.8 = (f32[64,256]{1,0:T(8,128)}, f32[64,256]{1,0:T(8,128)S(1)}, u32[]{:S(2)}, u32[]{:S(2)}) collective-permute-start(f32[64,256]{1,0:T(8,128)} %bitcast.20), channel_id=1, source_target_pairs={{0,4},{1,5},{2,6},{3,7},{4,0},{5,1},{6,2},{7,3},{8,12},{9,13},{10,... | collective-permute-start | bytes 196616 | tf_op jit(solution)/shard_map/ppermute | solution.py:26
  16.2 7.3 %collective-permute-start.5 = (f32[64,256]{1,0:T(8,128)S(1)}, f32[64,256]{1,0:T(8,128)S(1)}, u32[]{:S(2)}, u32[]{:S(2)}) collective-permute-start(f32[64,256]{1,0:T(8,128)S(1)} %get-tuple-element.21), channel_id=1, source_target_pairs={{0,2},{1,3},{2,0},{3,1},{4,6},{5,7},{6,4},{7,5},{8,10},{9,11},{10,... | collective-permute-start | bytes 196616 | tf_op jit(solution)/shard_map/ppermute | solution.py:26
  19.0 4.5 %collective-permute-start.6 = (f32[64,256]{1,0:T(8,128)S(1)}, f32[64,256]{1,0:T(8,128)S(1)}, u32[]{:S(2)}, u32[]{:S(2)}) collective-permute-start(f32[64,256]{1,0:T(8,128)S(1)} %get-tuple-element.22), channel_id=1, source_target_pairs={{0,3},{1,0},{2,1},{3,2},{4,7},{5,4},{6,5},{7,6},{8,11},{9,8},{10,9... | collective-permute-start | bytes 196616 | tf_op jit(solution)/shard_map/ppermute | solution.py:26
  19.9 4.3 %collective-permute-start.4 = (f32[64,256]{1,0:T(8,128)S(1)}, f32[64,256]{1,0:T(8,128)S(1)}, u32[]{:S(2)}, u32[]{:S(2)}) collective-permute-start(f32[64,256]{1,0:T(8,128)S(1)} %get-tuple-element.20), channel_id=1, source_target_pairs={{0,1},{1,2},{2,3},{3,0},{4,5},{5,6},{6,7},{7,4},{8,9},{9,10},{10,1... | collective-permute-start | bytes 196616 | tf_op jit(solution)/shard_map/ppermute | solution.py:26
  21.3 11.8 %collective-permute-start.11 = (f32[2,64,256]{2,1,0:T(8,128)S(1)}, f32[2,64,256]{2,1,0:T(8,128)S(1)}, u32[]{:S(2)}, u32[]{:S(2)}) collective-permute-start(f32[2,64,256]{2,1,0:T(8,128)S(1)} %pad_maximum_fusion.1.refs_0_), channel_id=1, source_target_pairs={{0,3},{1,0},{2,1},{3,2},{4,7},{5,4},{6,5},{7,6},{8,11},{9,8},{10,9... | collective-permute-start | bytes 393224 | tf_op jit(solution)/shard_map/ppermute | solution.py:26
  24.2 18.2 %collective-permute-start.7 = (f32[4,64,256]{2,1,0:T(8,128)S(1)}, f32[4,64,256]{2,1,0:T(8,128)S(1)}, u32[]{:S(2)}, u32[]{:S(2)}) collective-permute-start(f32[4,64,256]{2,1,0:T(8,128)S(1)} %pad_maximum_fusion.refs_0_), channel_id=1, source_target_pairs={{0,144},{1,145},{2,146},{3,147},{4,148},{5,149},{6,150},{7,151},{8... | collective-permute-start | bytes 786440 | tf_op jit(solution)/shard_map/ppermute | solution.py:26
  30.8 11.6 %collective-permute-start.13 = (f32[4,64,256]{2,1,0:T(8,128)S(1)}, f32[4,64,256]{2,1,0:T(8,128)S(1)}, u32[]{:S(2)}, u32[]{:S(2)}) collective-permute-start(f32[4,64,256]{2,1,0:T(8,128)S(1)} %pad_maximum_fusion.refs_0_), channel_id=1, source_target_pairs={{0,16},{1,17},{2,18},{3,19},{4,20},{5,21},{6,22},{7,23},{8,120},{9... | collective-permute-start | bytes 786440 | tf_op jit(solution)/shard_map/ppermute | solution.py:26
  32.2 11.7 %collective-permute-start.12 = (f32[4,64,256]{2,1,0:T(8,128)S(1)}, f32[4,64,256]{2,1,0:T(8,128)S(1)}, u32[]{:S(2)}, u32[]{:S(2)}) collective-permute-start(f32[4,64,256]{2,1,0:T(8,128)S(1)} %pad_maximum_fusion.refs_0_), channel_id=1, source_target_pairs={{0,128},{1,129},{2,130},{3,131},{4,132},{5,133},{6,134},{7,135},{8... | collective-permute-start | bytes 786440 | tf_op jit(solution)/shard_map/ppermute | solution.py:26
  32.2 5.6 %collective-permute-start.10 = (f32[2,64,256]{2,1,0:T(8,128)S(1)}, f32[2,64,256]{2,1,0:T(8,128)S(1)}, u32[]{:S(2)}, u32[]{:S(2)}) collective-permute-start(f32[2,64,256]{2,1,0:T(8,128)S(1)} %pad_maximum_fusion.1.refs_0_), channel_id=1, source_target_pairs={{0,2},{1,3},{2,0},{3,1},{4,6},{5,7},{6,4},{7,5},{8,10},{9,11},{10,... | collective-permute-start | bytes 393224 | tf_op jit(solution)/shard_map/ppermute | solution.py:26
  33.1 8.5 %collective-permute-start.9 = (f32[2,64,256]{2,1,0:T(8,128)S(1)}, f32[2,64,256]{2,1,0:T(8,128)S(1)}, u32[]{:S(2)}, u32[]{:S(2)}) collective-permute-start(f32[2,64,256]{2,1,0:T(8,128)S(1)} %pad_maximum_fusion.1.refs_0_), channel_id=1, source_target_pairs={{0,1},{1,2},{2,3},{3,0},{4,5},{5,6},{6,7},{7,4},{8,9},{9,10},{10,1... | collective-permute-start | bytes 393224 | tf_op jit(solution)/shard_map/ppermute | solution.py:26
  37.8 6.6 %collective-permute-start.14 = (f32[4,64,256]{2,1,0:T(8,128)S(1)}, f32[4,64,256]{2,1,0:T(8,128)S(1)}, u32[]{:S(2)}, u32[]{:S(2)}) collective-permute-start(f32[4,64,256]{2,1,0:T(8,128)S(1)} %pad_maximum_fusion.refs_0_), channel_id=1, source_target_pairs={{0,8},{1,9},{2,10},{3,11},{4,12},{5,13},{6,14},{7,15},{8,0},{9,1},... | collective-permute-start | bytes 786440 | tf_op jit(solution)/shard_map/ppermute | solution.py:26
  42.4 2.5 %collective-permute-start.16 = (f32[4,64,256]{2,1,0:T(8,128)S(1)}, f32[4,64,256]{2,1,0:T(8,128)S(1)}, u32[]{:S(2)}, u32[]{:S(2)}) collective-permute-start(f32[4,64,256]{2,1,0:T(8,128)S(1)} %collective-permute-done.13.refs_2_), channel_id=1, source_target_pairs={{0,8},{1,9},{2,10},{3,11},{4,12},{5,13},{6,14},{7,15},{8,0},{9,1},... | collective-permute-start | bytes 786440 | tf_op jit(solution)/shard_map/ppermute | solution.py:26
  43.8 1.5 %collective-permute-start.15 = (f32[4,64,256]{2,1,0:T(8,128)S(1)}, f32[4,64,256]{2,1,0:T(8,128)S(1)}, u32[]{:S(2)}, u32[]{:S(2)}) collective-permute-start(f32[4,64,256]{2,1,0:T(8,128)S(1)} %collective-permute-done.12.refs_1_), channel_id=1, source_target_pairs={{0,8},{1,9},{2,10},{3,11},{4,12},{5,13},{6,14},{7,15},{8,0},{9,1},... | collective-permute-start | bytes 786440 | tf_op jit(solution)/shard_map/ppermute | solution.py:26
  44.0 1.9 %collective-permute-start.17 = (f32[4,64,256]{2,1,0:T(8,128)S(1)}, f32[4,64,256]{2,1,0:T(8,128)}, u32[]{:S(2)}, u32[]{:S(2)}) collective-permute-start(f32[4,64,256]{2,1,0:T(8,128)S(1)} %collective-permute-done.7.refs_3_), channel_id=1, source_target_pairs={{0,8},{1,9},{2,10},{3,11},{4,12},{5,13},{6,14},{7,15},{8,0},{9,1},... | collective-permute-start | bytes 786440 | tf_op jit(solution)/shard_map/ppermute | solution.py:26
  44.3 1.5 %copy-start.1 = (f32[1024]{0:T(1024)S(1)}, f32[1024]{0:T(1024)}, u32[]{:S(2)}) copy-start(f32[1024]{0:T(1024)} %param.5) | copy-start | bytes 12292
